TPU v7x, 32 devices: a whole 2x2x4 slice. The times are simulated.
32 devices in a mesh: row: 4 (over x, core), col: 8 (over z, y).
Axes of the slice: x: 2, y: 2, z: 4, core: 2. Of those that a mesh axis runs over, the one named last changes fastest.
Arguments:
- currents: float32 [8192, 256], P(('row', 'col')), may hold values from -6 to 6
- branch_owner: int32 [8192, 2], P(('row', 'col')), may hold values from 0 to 31, all different within a row; in each aligned block of 256 rows (0 to 255, 256 to 511, ...) at most 64 rows name the same one
- branch_slot: int32 [8192, 2], P(('row', 'col')), may hold values from 0 to 4095
- history: bfloat16 [4, 131072, 256], P(None, 'col'), may hold values from -6 to 6
- coefficients: bfloat16 [4096, 131072], P('row', 'col'), may hold values from -0.0234375 to 0.0234375
- delays: int32 [16, 512], P('row', 'col'), may hold values from 0 to 4
- slab_owner: int32 [8192, 2], P(('row', 'col')), may hold values from 0 to 31, all different within a row; in each aligned block of 256 rows (0 to 255, 256 to 511, ...) at most 64 rows name the same one
- slab_offset: int32 [8192, 2], P(('row', 'col')), may hold values from 0 to 127
Outputs:
- charge_now: bfloat16 [131072, 256], P('col')
- drops: float32 [8192, 256], P(('row', 'col'))
Inputs may be any that keep to these rules, and one draw needn't show every extreme that they name: `branch_owner`: the two ends of a branch have different owners; among the rows of one device no owner is named more than 64 times. `slab_owner`: the two ends of a slab branch have different owners; among the rows of one device no owner is named more than 64 times.
All inputs are finite; a program needn't handle non-finite values.
Results may differ from a plain program's by a relative error of at most 0.0015.
Values may be sent and summed in bfloat16 or wider, within the bound.
No kernel may reach another device: no remote copies, remote signals or barrier semaphores. Data moves between devices by JAX's collectives and lax.ppermute only.
A program may use at most 256 MiB of HBM per device.

v0:
```python
import jax
import jax.numpy as jnp
from jax import lax
from jax.sharding import PartitionSpec as P


def place_rows(target, slot_count, capacity):
    onehot = (target[:, None] == jnp.arange(slot_count, dtype=jnp.int32)[None, :]).astype(jnp.int32)
    ranks = jnp.sum(jnp.cumsum(onehot, axis=0) * onehot, axis=1) - 1
    return target * capacity + ranks


def local(
    currents, branch_owner, branch_slot, history, coefficients, delays, slab_owner, slab_offset
):
    row_count = lax.axis_size("row")
    col_count = lax.axis_size("col")
    device_count = row_count * col_count
    branch_rows, scenarios = currents.shape
    owned = history.shape[1] // row_count
    capacity = 8 * branch_rows // device_count
    slab_total = coefficients.shape[0] * row_count
    share = slab_total // device_count
    owners = jnp.concatenate([branch_owner[:, 0], branch_owner[:, 1]])
    slots = jnp.concatenate([branch_slot[:, 0], branch_slot[:, 1]])
    values = jnp.concatenate([-currents, currents], axis=0)
    target = owners % row_count * col_count + owners // row_count
    position = place_rows(target, device_count, capacity)
    send_values = (
        jnp.zeros((device_count * capacity, scenarios), jnp.float32).at[position].set(values)
    )
    send_slots = jnp.zeros((device_count * capacity,), jnp.int32).at[position].set(slots)
    recv_values, recv_slots = (
        lax.all_to_all(send_values, ("row", "col"), split_axis=0, concat_axis=0, tiled=True),
        lax.all_to_all(send_slots, ("row", "col"), split_axis=0, concat_axis=0, tiled=True),
    )
    increment = jax.ops.segment_sum(recv_values, recv_slots, num_segments=owned)
    my_row = lax.axis_index("row")
    own_past = lax.dynamic_slice_in_dim(history[0], my_row * owned, owned, 0)
    charge_own = (own_past.astype(jnp.float32) + increment).astype(jnp.bfloat16)
    row_blocks, col_blocks = delays.shape
    block_size = coefficients.shape[1] // col_blocks
    past_blocks = history.reshape(history.shape[0], col_blocks, block_size, scenarios)
    column_ids = jnp.arange(col_blocks, dtype=jnp.int32)[None, :]
    earlier = past_blocks[jnp.maximum(delays - 1, 0), column_ids]
    charge_col = lax.all_gather(charge_own, "row", axis=0, tiled=True)
    now_blocks = charge_col.reshape(col_blocks, block_size, scenarios)
    source = jnp.where((delays == 0)[:, :, None, None], now_blocks[None], earlier)
    source = source.reshape(row_blocks, col_blocks * block_size, scenarios)
    coef_rows = coefficients.reshape(row_blocks, block_size, coefficients.shape[1])
    partial_rows = jnp.einsum("rkc,rcs->rks", coef_rows, source, preferred_element_type=jnp.float32)
    partial_rows = partial_rows.reshape(row_blocks * block_size, scenarios)
    row_total = lax.psum(partial_rows, "col")
    potentials = lax.all_gather(row_total, "row", axis=0, tiled=True)
    slab_nodes = slab_owner * share + slab_offset
    drops = potentials[slab_nodes[:, 0]] - potentials[slab_nodes[:, 1]]
    return (charge_col, drops)


def solution(mesh):
    placed = (
        P(("row", "col"), None),
        P(("row", "col"), None),
        P(("row", "col"), None),
        P(None, "col", None),
        P("row", "col"),
        P("row", "col"),
        P(("row", "col"), None),
        P(("row", "col"), None),
    )
    return jax.shard_map(
        local,
        mesh=mesh,
        in_specs=placed,
        out_specs=(P("col", None), P(("row", "col"), None)),
        check_vma=False,
    )
```

profile of v0, /device:TPU:0, one launch (start us, length us, event | category | flops | bytes accessed | tf_op | source)
XLA Modules:
  0.0 344.5 jit_solution(16378914805592906665)
XLA Ops:
  7.2 0.8 fusion.21
  8.0 1.2 reduce-window.6
  9.1 0.2 slice_reduce_fusion
  9.4 0.1 fusion.6
  9.6 0.8 fusion.20
  10.3 2.5 scatter_custom_fusion
  12.8 0.7 all_to_all.14
  13.5 7.3 %all-to-all-start = ((s32[32,64,1]{1,2,0:T(1,128)}), s32[32,64,1]{1,2,0:T(1,128)S(1)}, u32[]{:S(2)}, u32[]{:S(2)}) async-start(s32[32,64,1]{1,2,0:T(1,128)} %bitcast.9), calls=%async_computation | async-start | bytes 32768 | tf_op jit(solution)/shard_map/all_to_all | solution.py:35
  20.8 1.0 neg.3
  21.7 4.1 %scatter_custom_fusion.1 = f32[2048,256]{1,0:T(8,128)} fusion(s32[512]{0:T(512)S(1)} %bitcast.63, f32[]{:T(128)} %constant.66.clone.1, f32[256,256]{1,0:T(8,128)} %param.8, f32[]{:T(128)} %constant.84, f32[256,256]{1,0:T(8,128)S(1)} %neg.3), kind=kCustom, calls=%fused_computation.8 | custom fusion | flops 131072 | bytes 2621448 | tf_op jit(solution)/shard_map/scatter | solution.py:30
  25.8 2.0 all-to-all-done
  27.8 3.9 %all-to-all-start.1 = ((f32[32,64,256]{2,1,0:T(8,128)}), f32[32,64,256]{2,1,0:T(8,128)S(1)}, u32[]{:S(2)}, u32[]{:S(2)}) async-start(f32[32,64,256]{2,1,0:T(8,128)} %bitcast.51), calls=%async_computation.1 | async-start | bytes 4194304 | tf_op jit(solution)/shard_map/all_to_all | solution.py:34
  31.7 7.1 %slice.27 = bf16[1,16384,256]{2,1,0:T(8,128)(2,1)} slice(bf16[4,16384,256]{2,1,0:T(8,128)(2,1)} %param.11), slice={[0:1], [0:16384], [0:256]} | slice | bytes 16777216 | tf_op jit(solution)/shard_map/slice | solution.py:39
  38.8 3.8 %bitcast_convert_fusion = f32[4096,256]{1,0:T(8,128)} fusion(bf16[1,16384,256]{2,1,0:T(8,128)(2,1)} %slice.27, s32[]{:T(128)S(6)} %select_n.71), kind=kLoop, calls=%fused_computation.7 | loop fusion | flops 1048576 | bytes 6291460 | tf_op jit(solution)/shard_map/convert_element_type | solution.py:40
  42.7 0.5 broadcast.279
  43.2 0.7 reduce.5
  44.0 37.8 %all-to-all-done.1 = f32[32,64,256]{2,1,0:T(8,128)S(1)} async-done(((f32[32,64,256]{2,1,0:T(8,128)}), f32[32,64,256]{2,1,0:T(8,128)S(1)}, u32[]{:S(2)}, u32[]{:S(2)}) %all-to-all-start.1) | async-done | bytes 2097184 | tf_op jit(solution)/shard_map/all_to_all | solution.py:34
  81.8 16.9 %scatter_fusion = f32[4096,256]{1,0:T(8,128)} fusion(f32[4096,256]{1,0:T(8,128)} %bitcast_convert_fusion, s32[2048]{0:T(1024)S(1)} %reshape.347, f32[2048,256]{1,0:T(8,128)S(1)} %bitcast.50), kind=kCustom, calls=%fused_computation.5 | custom fusion | flops 524288 | bytes 6299648 | tf_op jit(solution)/shard_map/scatter-add | solution.py:37
  98.7 3.7 %convert_element_type.17 = bf16[4096,256]{1,0:T(8,128)(2,1)} convert(f32[4096,256]{1,0:T(8,128)} %scatter_fusion) | non-fusion elementwise | flops 1048576 | bytes 6291456 | tf_op jit(solution)/shard_map/convert_element_type | solution.py:40
  102.5 0.1 reshape.307
  102.6 0.1 broadcast_bitcast_fusion
  102.7 0.1 copy.14
  102.8 24.2 %gather_fusion = bf16[256,256,256]{2,1,0:T(8,128)(2,1)} fusion(bf16[4,64,256,256]{3,2,1,0:T(8,128)(2,1)} %bitcast.49, s32[256]{0:T(256)S(1)} %reshape.307), kind=kCustom, calls=%fused_computation | custom fusion | bytes 67110912 | tf_op jit(solution)/shard_map/gather | solution.py:45
  127.0 32.7 %all-gather.3.cloned.1.call-done = bf16[16384,256]{1,0:T(8,128)(2,1)} async-done(((bf16[4096,256]{1,0:T(8,128)(2,1)}), bf16[16384,256]{1,0:T(8,128)(2,1)}) %all-gather.3.cloned.1.call-update) | async-done | bytes 8388624 | tf_op jit(solution)/shard_map/all_gather | solution.py:46
  159.7 25.8 %bitcast_select_fusion = bf16[4,16384,256]{2,1,0:T(8,128)(2,1)} fusion(pred[4,16384]{1,0:T(4,128)(4,1)S(1)} %bitcast.53, bf16[16384,256]{1,0:T(8,128)(2,1)} %all-gather.3.cloned.1.call-done, bf16[4,16384,256]{2,1,0:T(8,128)(2,1)} %bitcast.48), kind=kLoop, calls=%fused_computation.6 | loop fusion | flops 16777216 | bytes 75563008 | tf_op jit(solution)/shard_map/jit(_where)/select_n | solution.py:48
  185.4 24.4 %fusion.22 = f32[4,256,256]{1,2,0:T(8,128)} fusion(bf16[4,256,16384]{2,1,0:T(8,128)(2,1)} %bitcast.64, bf16[4,16384,256]{2,1,0:T(8,128)(2,1)} %bitcast_select_fusion), kind=kOutput, calls=%fused_computation.65 | convolution fusion | flops 8589934592 | bytes 68157440 | tf_op jit(solution)/shard_map/rkc,rcs->rks/dot_general | solution.py:51
  210.0 78.1 %all-reduce.2.cloned.1.call-done = f32[1024,256]{1,0:T(8,128)} async-done(((f32[1024,256]{1,0:T(8,128)}), f32[1024,256]{1,0:T(8,128)}) %all-reduce.2.cloned.1.call-update) | async-done | bytes 1048592 | tf_op jit(solution)/shard_map/psum | solution.py:53
  288.2 35.6 %all-gather.5.cloned.1.call-done = f32[4096,256]{1,0:T(8,128)} async-done(((f32[1024,256]{1,0:T(8,128)}), f32[4096,256]{1,0:T(8,128)}) %all-gather.5.cloned.1.call-update) | async-done | bytes 4194320 | tf_op jit(solution)/shard_map/all_gather | solution.py:54
  323.8 3.2 gather_fusion.1
  327.0 3.2 gather_fusion.2
  330.1 0.7 sub.29
  330.9 7.1 %copy.19 = bf16[16384,256]{1,0:T(8,128)(2,1)} copy(bf16[16384,256]{1,0:T(8,128)(2,1)} %all-gather.3.cloned.1.call-done) | data formatting | bytes 16777216
  (28 shorter events, 0.4 us)
Async XLA Ops:
  13.5 14.3 %all-to-all-start = ((s32[32,64,1]{1,2,0:T(1,128)}), s32[32,64,1]{1,2,0:T(1,128)S(1)}, u32[]{:S(2)}, u32[]{:S(2)}) async-start(s32[32,64,1]{1,2,0:T(1,128)} %bitcast.9), calls=%async_computation | async-start | bytes 32768 | tf_op jit(solution)/shard_map/all_to_all | solution.py:35
  27.8 54.0 %all-to-all-start.1 = ((f32[32,64,256]{2,1,0:T(8,128)}), f32[32,64,256]{2,1,0:T(8,128)S(1)}, u32[]{:S(2)}, u32[]{:S(2)}) async-start(f32[32,64,256]{2,1,0:T(8,128)} %bitcast.51), calls=%async_computation.1 | async-start | bytes 4194304 | tf_op jit(solution)/shard_map/all_to_all | solution.py:34
  31.7 128.0 %all-gather.3.cloned.1.call-start = ((), (), s32[]{:S(2)}) async-start(), calls=%async_computation.2 | async-start | bytes 10485760 | tf_op jit(solution)/shard_map/all_gather | solution.py:46
  98.7 3.8 %copy-start = (s32[4,64]{1,0:T(4,128)S(1)}, s32[4,64]{1,0:T(4,128)}, u32[]{:S(2)}) copy-start(s32[4,64]{1,0:T(4,128)} %param.13) | copy-start | bytes 3076
  102.4 185.7 %all-reduce.2.cloned.1.call-start = ((), (), s32[]{:S(2)}) async-start(), calls=%async_computation.3 | async-start | bytes 2097152 | tf_op jit(solution)/shard_map/psum | solution.py:53
  185.4 102.7 %copy-start.1 = (s32[256,2]{0,1:T(2,128)S(1)}, s32[256,2]{0,1:T(2,128)}, u32[]{:S(2)}) copy-start(s32[256,2]{0,1:T(2,128)} %param.15) | copy-start | bytes 6148
  185.4 102.7 %copy-start.2 = (s32[256,2]{0,1:T(2,128)S(1)}, s32[256,2]{0,1:T(2,128)}, u32[]{:S(2)}) copy-start(s32[256,2]{0,1:T(2,128)} %param.14) | copy-start | bytes 6148
  209.9 113.9 %all-gather.5.cloned.1.call-start = ((), (), s32[]{:S(2)}) async-start(), calls=%async_computation.4 | async-start | bytes 5242880 | tf_op jit(solution)/shard_map/all_gather | solution.py:54
Sparse Core Ops, SparseCore 0:
  102.5 57.0 all-gather.2
  210.0 78.0 all-reduce.1
  289.7 34.0 all-gather.4
where the time goes:
time: 345 us
  waiting for transfers between devices  186 us (54%)
  other arithmetic  58.1 us (17%)
  local copies, waits for them, and re-layouts  50.5 us (15%)
  matrix products  24.4 us (7%)
  between operations  13.9 us (4%)
  starting transfers between devices  11.3 us (3%)
    psum x1, waiting for transfers between devices, local(): row_total = lax.psum(partial_rows, 'col')  78.1 us
    all_to_all x1, waiting for transfers between devices, local(): lax.all_to_all(send_values, ('row', 'col'), split_axis=0, concat_axis=0,...  37.8 us
    all_gather x1, waiting for transfers between devices, local(): potentials = lax.all_gather(row_total, 'row', axis=0, tiled=True)  35.6 us
    all_gather x1, waiting for transfers between devices, local(): charge_col = lax.all_gather(charge_own, 'row', axis=0, tiled=True)  32.7 us
    select_n x1, other arithmetic, local(): jnp.where((delays == 0)[:, :, None, None], now_blocks[None], earlier)  25.8 us
    dot_general x1, matrix products, local(): jnp.einsum('rkc,rcs->rks', coef_rows, source, preferred_element_type=jnp....  24.4 us
    gather x1, local copies, waits for them, and re-layouts, local(): earlier = past_blocks[jnp.maximum(delays - 1, 0), column_ids]  24.2 us
    scatter-add x1, other arithmetic, local(): increment = jax.ops.segment_sum(recv_values, recv_slots, num_segments=owned)  16.9 us
  transfers between devices with their start and end apart: 5, of which 5 were waited for; matrix products, arithmetic and copies ran while one was open for 12% of the time, Pallas kernels for 0%

commit v1 on v0

v1 whole, which is shorter than its diff:
```python
import functools

import jax
import jax.numpy as jnp
import numpy as np
from jax import lax
from jax.experimental import pallas as pl
from jax.experimental.pallas import tpu as pltpu
from jax.sharding import PartitionSpec as P

F32, BF16, I32 = jnp.float32, jnp.bfloat16, jnp.int32
ALL = ("row", "col")
CHAINS = 4
UNROLL = 2
LANES = 128
FULL = 32767.0
LOW = 107
SIGNS = 9
MEAN = float(1 << 30)


def log2(n):
    bits = int(n).bit_length() - 1
    assert 1 << bits == n
    return bits


def powers():
    lane = lax.broadcasted_iota(I32, (1, LANES), 1)
    up = jnp.full((1, LANES), 2.0**-LOW, F32)
    down = jnp.full((1, LANES), 2.0**LOW, F32)
    for bit in range(log2(LANES)):
        on = lax.bitwise_and(lane, 1 << bit) > 0
        up = jnp.where(on, up * 2.0 ** (1 << bit), up)
        down = jnp.where(on, down * 2.0 ** -(1 << bit), down)
    return up, down


def signed_steps():
    up = np.ldexp(1 / np.float64(FULL), np.arange(LANES) - LOW)
    table = np.zeros(512, np.float32)
    table[1 : LANES + 1] = up
    table[LANES + 1 : 2 * LANES + 1] = -up
    return jnp.asarray(table)


def scale_of(values, up, down):
    most = jnp.max(jnp.abs(values), axis=1, keepdims=True)
    fits = up >= most
    inverse = jnp.max(jnp.where(fits, down, 0.0), axis=1, keepdims=True)
    index = jnp.sum(jnp.where(fits, 0, 1), axis=1, keepdims=True)
    return index, inverse


def coded(values, inverse):
    return jnp.floor(values * (inverse * FULL) + 0.5).astype(I32)


def pair(low, high):
    return lax.bitwise_or(lax.shift_left(high, 16), lax.bitwise_and(low, 0xFFFF))


def low_of(words):
    return lax.shift_right_arithmetic(lax.shift_left(words, 16), 16)


def high_of(words):
    return lax.shift_right_arithmetic(words, 16)


def vmem(n=1):
    return [pl.BlockSpec(memory_space=pltpu.VMEM)] * n


def params(mib, **more):
    return pltpu.CompilerParams(vmem_limit_bytes=mib << 20, **more)


def pack_kernel(current_ref, out_ref):
    values = current_ref[...]
    _, inverse = scale_of(values, *powers())
    codes = coded(values, inverse)
    half = codes.shape[1] // 2
    out_ref[...] = pair(codes[:, :half], codes[:, half:])


def pack(currents):
    rows, scenarios = currents.shape
    return pl.pallas_call(
        pack_kernel,
        out_shape=jax.ShapeDtypeStruct((rows, scenarios // 2), I32),
        in_specs=vmem(1),
        out_specs=vmem()[0],
        compiler_params=params(16),
        name="pack",
    )(currents)


def list_kernel(sizes, current_ref, owner_ref, slot_ref, out_ref, tally_ref):
    rows_of, owned, block, capacity, chain_rows = sizes
    index, _ = scale_of(current_ref[...], *powers())
    count = current_ref.shape[0]
    owner = jnp.concatenate([owner_ref[:, 0:1], owner_ref[:, 1:2]], axis=0)
    slot = jnp.concatenate([slot_ref[:, 0:1], slot_ref[:, 1:2]], axis=0)
    step = jnp.concatenate([index + (LANES + 1), index + 1], axis=0)
    branch = lax.broadcasted_iota(I32, (count, 1), 0)
    branch = jnp.concatenate([branch, branch], axis=0)
    column = lax.shift_right_logical(owner, log2(rows_of))
    node = lax.bitwise_and(owner, rows_of - 1) * owned + slot
    at_block = lax.shift_right_logical(node, log2(block))
    chain = lax.bitwise_and(at_block, CHAINS - 1)
    place = lax.shift_right_logical(at_block, log2(CHAINS)) * block
    place = place + lax.bitwise_and(node, block - 1)
    entry = step + lax.shift_left(place, SIGNS)
    entry = entry + lax.shift_left(branch, SIGNS + log2(chain_rows))
    key = column * CHAINS + chain
    ends = 2 * count
    hit = key == lax.broadcasted_iota(I32, (ends, LANES), 1)
    onehot = jnp.where(hit, 1.0, 0.0).astype(BF16)
    before = lax.broadcasted_iota(I32, (ends, ends), 0) > lax.broadcasted_iota(I32, (ends, ends), 1)
    before = jnp.where(before, 1.0, 0.0).astype(BF16)
    ranks = jnp.dot(before, onehot, preferred_element_type=F32)
    rank = jnp.sum(jnp.where(hit, ranks, 0.0), axis=1, keepdims=True).astype(I32)
    placed = rank == lax.broadcasted_iota(I32, (ends, capacity), 1)
    contract = (((0,), (0,)), ((), ()))
    total = jnp.zeros((LANES, capacity), I32)
    for piece in range(4):
        part = lax.bitwise_and(lax.shift_right_logical(entry, 8 * piece), 255)
        part = jnp.where(placed, part.astype(F32), 0.0).astype(BF16)
        found = lax.dot_general(onehot, part, contract, preferred_element_type=F32)
        total = total + lax.shift_left(found.astype(I32), 8 * piece)
    tally_ref[...] = jnp.sum(jnp.where(hit, 1, 0), axis=0, keepdims=True)
    out_ref[...] = total[: out_ref.shape[0]]


def make_lists(currents, owner, slot, sizes, keys):
    return pl.pallas_call(
        functools.partial(list_kernel, sizes),
        out_shape=(jax.ShapeDtypeStruct((keys, sizes[3]), I32), jax.ShapeDtypeStruct((1, LANES), I32)),
        in_specs=vmem(3),
        out_specs=tuple(vmem(2)),
        compiler_params=params(24),
        name="lists",
    )(currents, owner, slot)


def routes(row_count, col_count):
    col_bits, row_bits = log2(col_count), log2(row_count)
    across = [1 << b for b in (*range(1, col_bits), *([0] if col_bits else []))]
    along = [1 << (b + col_bits) for b in range(1, row_bits)]
    return (across + along, along + across), 1 << col_bits


def masks(steps):
    found = [0]
    for step in steps:
        found = found + [m ^ step for m in found]
    return found


def positions(row_count, col_count):
    orders, core = routes(row_count, col_count)
    devices = row_count * col_count
    table = np.zeros((devices, devices), np.int32)
    for me in range(devices):
        for far, holder in enumerate((me, me ^ core)):
            order = orders[1 if holder & core else 0]
            for at, mask in enumerate(masks(order)):
                table[me, holder ^ mask] = far * (devices // 2) + at
    return table


def gather_steps(row_count, col_count):
    orders, core = routes(row_count, col_count)
    devices = row_count * col_count
    pairs = []
    for first, second in zip(*orders):
        pairs.append([(d, d ^ (second if d & core else first)) for d in range(devices)])
    sibling = [(d, d ^ core) for d in range(devices)]
    return pairs, sibling


def past_kernel(span, block, first, delays_ref, coef_ref, history_ref, start_ref, out_ref, source):
    step = pl.program_id(0)

    @pl.when(step == 0)
    def _():
        out_ref[...] = start_ref[...]

    for i in range(delays_ref.shape[0]):
        for g in range(span):
            delay = delays_ref[i, first + step * span + g]
            at = pl.ds(g * block, block)
            held = history_ref[jnp.maximum(delay - 1, 0), at, :]
            source[i % 2, at, :] = jnp.where(delay > 0, held, jnp.zeros_like(held))
        rows = pl.ds(i * block, block)
        out_ref[rows, :] += jnp.dot(coef_ref[rows, :], source[i % 2], preferred_element_type=F32)


def past_product(delays, coefficients, history, start, block, first, blocks):
    span = 4
    rows = coefficients.shape[0]
    steps, scenarios = history.shape[0], history.shape[2]
    moved = (rows * 2 + steps * scenarios * 2) * block * blocks + 8 * rows * scenarios
    return pl.pallas_call(
        functools.partial(past_kernel, span, block, first),
        out_shape=jax.ShapeDtypeStruct((rows, scenarios), F32),
        grid=(blocks // span,),
        in_specs=[
            pl.BlockSpec(memory_space=pltpu.SMEM),
            pl.BlockSpec((rows, span * block), lambda k: (0, first // span + k)),
            pl.BlockSpec((steps, span * block, scenarios), lambda k: (0, first // span + k, 0)),
            pl.BlockSpec((rows, scenarios), lambda k: (0, 0)),
        ],
        out_specs=pl.BlockSpec((rows, scenarios), lambda k: (0, 0)),
        scratch_shapes=[pltpu.VMEM((2, span * block, scenarios), BF16)],
        compiler_params=params(32),
        cost_estimate=pl.CostEstimate(
            flops=2 * rows * block * blocks * scenarios, bytes_accessed=moved, transcendentals=0
        ),
        name="past",
    )(delays, coefficients, history, start)


def now_kernel(
    sizes,
    lists_ref, base_ref, tally_ref, table_ref, delays_ref, past_ref,
    near_ref, mid_ref, far_ref, last_ref, history_ref, coef_ref,
    charge_ref, out_ref,
    rows, acc, charge, coef, total, todo, row_sem, load_sem, store_sem, coef_sem,
):
    block, capacity, words, slots, chunks = sizes
    devices = base_ref.shape[0]
    row_blocks, col_blocks = delays_ref.shape
    chain_rows = acc.shape[2]
    quarter = rows.shape[0] // 4
    pieces = (near_ref, mid_ref, far_ref, last_ref)
    row_copies = [
        pltpu.make_async_copy(piece, rows.at[pl.ds(n * quarter, quarter)], row_sem.at[n])
        for n, piece in enumerate(pieces)
    ]
    for copy in row_copies:
        copy.start()
    load = pltpu.make_async_copy(history_ref.at[0], charge, load_sem)
    load.start()

    def scan(at, found):
        i = at // col_blocks
        k = at % col_blocks

        @pl.when(delays_ref[i, k] == 0)
        def _():
            todo[found] = at

        return found + jnp.where(delays_ref[i, k] == 0, 1, 0)

    count = lax.fori_loop(0, row_blocks * col_blocks, scan, jnp.int32(0))

    def coef_copy(t):
        at = todo[t]
        i = at // col_blocks
        k = at % col_blocks
        slot = lax.rem(t, slots)
        return pltpu.make_async_copy(
            coef_ref.at[pl.ds(pl.multiple_of(i * block, block), block),
                        pl.ds(pl.multiple_of(k * block, block), block)],
            coef.at[slot],
            coef_sem.at[slot],
        )

    @pl.loop(0, jnp.minimum(count, slots))
    def _(t):
        coef_copy(t).start()

    for chain in range(CHAINS):
        for side in range(2):
            @pl.loop(0, chain_rows // block)
            def _(n):
                at = pl.ds(pl.multiple_of(n * block, block), block)
                acc[chain * 2 + side][at, :] = jnp.zeros((block, LANES), F32)

    for copy in row_copies:
        copy.wait()

    row_shift = SIGNS + log2(chain_rows)

    @pl.loop(0, devices)
    def _(source):
        base = base_ref[source]
        start = source * words
        most = tally_ref[source]

        @pl.loop(0, (most + (UNROLL - 1)) // UNROLL)
        def _(j):
            for u in range(UNROLL):
                for chain in range(CHAINS):
                    entry = lists_ref[start + chain * capacity + j * UNROLL + u]
                    row = base + lax.shift_right_logical(entry, row_shift)
                    place = lax.bitwise_and(lax.shift_right_logical(entry, SIGNS), chain_rows - 1)
                    step = table_ref[lax.bitwise_and(entry, (1 << SIGNS) - 1)]
                    word = rows[pl.ds(row, 1), :]
                    at = pl.ds(place, 1)
                    acc[chain * 2][at, :] += low_of(word).astype(F32) * step
                    acc[chain * 2 + 1][at, :] += high_of(word).astype(F32) * step

    load.wait()

    def store(k):
        at = pl.ds(pl.multiple_of(k * block, block), block)
        return pltpu.make_async_copy(charge.at[at], charge_ref.at[at], store_sem)

    @pl.loop(0, col_blocks // CHAINS)
    def _(group):
        held = pl.ds(pl.multiple_of(group * block, block), block)
        for chain in range(CHAINS):
            k = group * CHAINS + chain
            at = pl.ds(pl.multiple_of(k * block, block), block)
            for side in range(2):
                lanes = slice(side * LANES, (side + 1) * LANES)
                charge[at, lanes] = (charge[at, lanes].astype(F32) + acc[chain * 2 + side][held, :]).astype(BF16)
            store(k).start()

    for i in range(row_blocks):
        total[i] = past_ref[i * block : (i + 1) * block, :]

    @pl.loop(0, count)
    def _(t):
        at = todo[t]
        i = at // col_blocks
        k = at % col_blocks
        slot = lax.rem(t, slots)
        coef_copy(t).wait()
        source = charge[pl.ds(pl.multiple_of(k * block, block), block), :]
        total[i] += jnp.dot(coef[slot], source, preferred_element_type=F32)

        @pl.when(t + slots < count)
        def _():
            coef_copy(t + slots).start()

    turned = jnp.concatenate([total[i].T for i in range(row_blocks)], axis=1)
    up, down = powers()
    nodes = turned.shape[1]
    mean = jnp.sum(turned, axis=1, keepdims=True) * (1.0 / nodes)
    rest = turned - mean
    index, inverse = scale_of(rest, up, down)
    codes = coded(rest, inverse)
    mean_index, mean_inverse = scale_of(mean, up, down)
    mean_code = jnp.floor(mean * mean_inverse * MEAN).astype(I32)
    lane = lax.broadcasted_iota(I32, (turned.shape[0], LANES), 1)
    head = jnp.where(lane == 0, index, jnp.where(lane == 1, mean_index, jnp.where(lane == 2, mean_code, 0)))
    chunk = turned.shape[0] // chunks
    half = chunk // 2
    for c in range(chunks):
        one = slice(c * chunk, c * chunk + half)
        two = slice(c * chunk + half, (c + 1) * chunk)
        out_ref[c, :, :nodes] = pair(codes[one], codes[two])
        out_ref[c, :, nodes : nodes + LANES] = head[one]
        out_ref[c, :, nodes + LANES :] = head[two]

    pltpu.make_async_copy(charge, charge_ref, store_sem).wait()


def now_product(lists, base, tally, table, delays, past, pieces, history, coefficients, block, capacity, words, chunks):
    rows, scenarios = past.shape
    nodes = history.shape[1]
    row_blocks, col_blocks = delays.shape
    slots = 32
    smem = pl.BlockSpec(memory_space=pltpu.SMEM)
    hbm = pl.BlockSpec(memory_space=pl.ANY)
    sizes = (block, capacity, words, slots, chunks)

    def kernel(*refs):
        refs = list(refs)
        at = 14
        acc = refs[at + 1 : at + 1 + 2 * CHAINS]
        now_kernel(sizes, *refs[: at + 1], ListOf(acc), *refs[at + 1 + 2 * CHAINS :])

    return pl.pallas_call(
        kernel,
        out_shape=(
            jax.ShapeDtypeStruct((nodes, scenarios), BF16),
            jax.ShapeDtypeStruct((chunks, scenarios // chunks // 2, rows + 2 * LANES), I32),
        ),
        in_specs=[smem] * 5 + vmem(1) + [hbm] * 6,
        out_specs=(hbm, vmem()[0]),
        scratch_shapes=[
            pltpu.VMEM((4 * pieces[0].shape[0], scenarios // 2), I32),
            *[pltpu.VMEM((nodes // CHAINS, LANES), F32) for _ in range(2 * CHAINS)],
            pltpu.VMEM((nodes, scenarios), BF16),
            pltpu.VMEM((slots, block, block), BF16),
            pltpu.VMEM((row_blocks, block, scenarios), F32),
            pltpu.SMEM((row_blocks * col_blocks,), I32),
            pltpu.SemaphoreType.DMA((4,)),
            pltpu.SemaphoreType.DMA,
            pltpu.SemaphoreType.DMA,
            pltpu.SemaphoreType.DMA((slots,)),
        ],
        compiler_params=params(60),
        cost_estimate=pl.CostEstimate(flops=1 << 30, bytes_accessed=80 << 20, transcendentals=0),
        name="now",
    )(lists, base, tally, table, delays, past, *pieces, history, coefficients)


class ListOf(list):
    @property
    def shape(self):
        return (len(self), 1, self[0].shape[0], self[0].shape[1])


def sum_kernel(got_ref, out_ref):
    sources, half, width = got_ref.shape
    nodes = width - 2 * LANES
    up, _ = powers()
    lane = lax.broadcasted_iota(I32, (half, LANES), 1)

    def power(index):
        return jnp.sum(jnp.where(lane == index, up, 0.0), axis=1, keepdims=True)

    for side in range(2):
        total = jnp.zeros((half, nodes), F32)
        for source in range(sources):
            words = got_ref[source, :, :nodes]
            head = got_ref[source, :, nodes + side * LANES : nodes + (side + 1) * LANES]
            codes = (high_of(words) if side else low_of(words)).astype(F32)
            mean = head[:, 2:3].astype(F32) * (power(head[:, 1:2]) * (1.0 / MEAN))
            total = total + (codes * (power(head[:, 0:1]) * (1.0 / FULL)) + mean)
        out_ref[side * half : (side + 1) * half, :] = total


def sum_columns(got):
    _, half, width = got.shape
    return pl.pallas_call(
        sum_kernel,
        out_shape=jax.ShapeDtypeStruct((2 * half, width - 2 * LANES), F32),
        in_specs=vmem(1),
        out_specs=vmem()[0],
        compiler_params=params(16),
        name="sum",
    )(got)


def drop_kernel(node_ref, potential_ref, out_ref):
    row_count, excitations, nodes = potential_ref.shape
    per_row = nodes // LANES
    groups = excitations // 8

    @pl.loop(0, node_ref.shape[1] // LANES)
    def _(group):
        at = pl.ds(pl.multiple_of(group * LANES, LANES), LANES)
        found = [[None] * groups, [None] * groups]
        for end in range(2):
            node = jnp.broadcast_to(node_ref[pl.ds(end, 1), at], (8, LANES))
            inner = lax.bitwise_and(node, LANES - 1)
            outer = lax.shift_right_logical(node, log2(LANES))
            for e in range(groups):
                value = jnp.zeros((8, LANES), F32)
                for h in range(row_count * per_row):
                    lanes = slice(h % per_row * LANES, (h % per_row + 1) * LANES)
                    held = potential_ref[h // per_row, e * 8 : (e + 1) * 8, lanes]
                    seen = jnp.take_along_axis(held, inner, axis=1, mode="promise_in_bounds")
                    value = jnp.where(outer == h, seen, value)
                found[end][e] = value
        for e in range(groups):
            out_ref[e * 8 : (e + 1) * 8, at] = found[0][e] - found[1][e]


def row_drops(nodes, potentials):
    return pl.pallas_call(
        drop_kernel,
        out_shape=jax.ShapeDtypeStruct((potentials.shape[1], nodes.shape[1]), F32),
        in_specs=vmem(2),
        out_specs=vmem()[0],
        compiler_params=params(24),
        name="drops",
    )(nodes, potentials)


def branch_lists(currents, owner, slot, slab_owner, slab_offset, col_count, share, sizes):
    lists, tally = make_lists(currents, owner, slot, sizes, col_count * CHAINS)
    slab = (slab_owner * share + slab_offset).T.reshape(-1, LANES)
    return lists.reshape(col_count, -1, LANES), tally, slab


def share_lists(lists, tally, slab, row_count, col_count):
    common = jnp.concatenate([tally, slab], axis=0)
    extra = -(lists.shape[1] + common.shape[0]) % 8
    common = jnp.concatenate([common, jnp.zeros((extra, LANES), I32)], axis=0)
    common = jnp.broadcast_to(common[None], (col_count, *common.shape))
    message = jnp.concatenate([lists, common], axis=1)
    message = jnp.broadcast_to(message[None], (row_count, *message.shape)).reshape(-1, LANES)
    return lax.all_to_all(message, ALL, split_axis=0, concat_axis=0, tiled=True)


def local(currents, branch_owner, branch_slot, history, coefficients, delays, slab_owner, slab_offset):
    row_count = lax.axis_size("row")
    col_count = lax.axis_size("col")
    devices = row_count * col_count
    branch_rows, scenarios = currents.shape
    owned = history.shape[1] // row_count
    block = coefficients.shape[1] // delays.shape[1]
    per_owner = 8 * branch_rows // devices
    capacity = -(-min(2 * branch_rows, row_count * per_owner) // LANES) * LANES
    chain_rows = history.shape[1] // CHAINS
    share = coefficients.shape[0] * row_count // devices
    my_row, my_col = lax.axis_index("row"), lax.axis_index("col")
    me = my_row * col_count + my_col
    pairs, sibling = gather_steps(row_count, col_count)
    parts = 4
    col_blocks = delays.shape[1]
    past = jnp.zeros((coefficients.shape[0], scenarios), F32)
    together = lax.optimization_barrier

    def add_past(past, part):
        return past_product(
            delays, coefficients, history, past, block, part * col_blocks // parts, col_blocks // parts
        )

    held = pack(currents)
    jobs = {0: (), 1: (0,), 2: (1,), 3: (2, 3)}
    message = None
    for number, step in enumerate(pairs[:-1]):
        held, past, currents = together((held, past, currents))
        got = lax.ppermute(held, ALL, step)
        for job in jobs.get(number, ()):
            past = add_past(past, job)
        if number == 0:
            lists, tally, slab = branch_lists(
                currents, branch_owner, branch_slot, slab_owner, slab_offset, col_count, share,
                (row_count, owned, block, capacity, chain_rows),
            )
            got, past, lists, tally, slab = together((got, past, lists, tally, slab))
            message = share_lists(lists, tally, slab, row_count, col_count)
        elif number == 2:
            got, past, message = together((got, past, message))
        else:
            got, past = together((got, past))
        held = jnp.concatenate([held, got], axis=0)
    held, past = together((held, past))
    mid = lax.ppermute(held, ALL, pairs[-1])
    far = lax.ppermute(held, ALL, sibling)
    for number in range(len(pairs) - 1, parts):
        for job in jobs[number]:
            past = add_past(past, job)
    mid, past = together((mid, past))
    last = lax.ppermute(mid, ALL, sibling)

    list_tiles = CHAINS * capacity // LANES
    slab_rows = slab_owner.shape[0]
    slab_tiles = 2 * slab_rows // LANES
    width = message.shape[0] // devices
    message = message.reshape(devices, width, LANES)
    tally = lax.dynamic_slice_in_dim(message[:, list_tiles], my_col * CHAINS, CHAINS, 1).max(axis=1)
    row_slab = lax.dynamic_slice_in_dim(message, my_row * col_count, col_count, 0)
    row_slab = row_slab[:, list_tiles + 1 : list_tiles + 1 + slab_tiles]
    row_slab = row_slab.reshape(col_count, 2, slab_rows).transpose(1, 0, 2).reshape(2, col_count * slab_rows)
    table = jnp.asarray(positions(row_count, col_count) * branch_rows)
    base = lax.dynamic_slice_in_dim(table, me, 1, 0)[0]

    charge, partial = now_product(
        message.reshape(-1), base, tally, signed_steps(), delays, past, (held, mid, far, last),
        history, coefficients, block, capacity, width * LANES, col_count,
    )

    got = lax.all_to_all(partial, "col", split_axis=0, concat_axis=0, tiled=True)
    mine = sum_columns(got)
    potentials = lax.all_gather(mine, "row", axis=0, tiled=False)
    found = row_drops(row_slab, potentials)
    excitations = found.shape[0]
    found = found.reshape(excitations, col_count, slab_rows).transpose(1, 0, 2)
    found = lax.all_to_all(found, "col", split_axis=0, concat_axis=0, tiled=True)
    return charge, found.reshape(col_count * excitations, slab_rows).T


def solution(mesh):
    both = P(("row", "col"), None)
    placed = (both, both, both, P(None, "col", None), P("row", "col"), P("row", "col"), both, both)
    return jax.shard_map(
        local,
        mesh=mesh,
        in_specs=placed,
        out_specs=(P("col", None), both),
        check_vma=False,
    )
```

time: 345 us -> 156 us (0.45)
  waiting for transfers between devices: 186 us -> 22.8 us
  Pallas kernels: 0 us -> 77.5 us
  other arithmetic: 58.1 us -> 2.23 us
  local copies, waits for them, and re-layouts: 50.5 us -> 9.87 us
  matrix products: 24.4 us -> 0 us
  blocking collectives: 0 us -> 21.5 us
  between operations: 13.9 us -> 0.84 us
  starting transfers between devices: 11.3 us -> 21.6 us
    psum x1 -> x0, waiting for transfers between devices: 78.1 us -> none  [local(): row_total = lax.psum(partial_rows, 'col')]
    pallas_call x0 -> x9, Pallas kernels: none -> 77.5 us  [the longest x1 37.9 us: now_product(): pl.pallas_call(kernel, out_shape=(jax.ShapeDtypeStruct((nodes, scenarios)...]
    all_gather x2 -> x0, waiting for transfers between devices: 68.3 us -> none  [the longest x1 35.6 us: local(): potentials = lax.all_gather(row_total, 'row', axis=0, tiled=True)]
    gather x3 -> x0, local copies, waits for them, and re-layouts: 30.5 us -> none  [the longest x1 24.2 us: local(): earlier = past_blocks[jnp.maximum(delays - 1, 0), column_ids]]
    select_n x3 -> x0, other arithmetic: 25.8 us -> none  [the longest x1 25.8 us: local(): jnp.where((delays == 0)[:, :, None, None], now_blocks[None], earlier)]
    dot_general x1 -> x0, matrix products: 24.4 us -> none  [local(): jnp.einsum('rkc,rcs->rks', coef_rows, source, preferred_element_type=jnp....]
    all_to_all x2, waiting for transfers between devices: 39.8 us -> 22.8 us  [the longest x1 16.2 us: local(): lax.all_to_all(partial, 'col', split_axis=0, concat_axis=0, tiled=True)]
    scatter-add x1 -> x0, other arithmetic: 16.9 us -> none  [local(): increment = jax.ops.segment_sum(recv_values, recv_slots, num_segments=owned)]
  transfers between devices with their start and end apart: 5 -> 8, of which waited for: 5 -> 2; matrix products, arithmetic and copies ran while one was open for 12% -> 4% of each run, Pallas kernels for 0% -> 20%
where the time goes in v1:
time: 156 us
  Pallas kernels  77.5 us (50%)
  waiting for transfers between devices  22.8 us (15%)
  starting transfers between devices  21.6 us (14%)
  blocking collectives  21.5 us (14%)
  local copies, waits for them, and re-layouts  9.87 us (6%)
  other arithmetic  2.23 us (1%)
    pallas_call x1, Pallas kernels, now_product(): pl.pallas_call(kernel, out_shape=(jax.ShapeDtypeStruct((nodes, scenarios)...  37.9 us
    pallas_call x4, Pallas kernels, past_product(): pl.pallas_call(functools.partial(past_kernel, span, block, first), out_sh...  30.6 us
    all_to_all x1, waiting for transfers between devices, local(): lax.all_to_all(partial, 'col', split_axis=0, concat_axis=0, tiled=True)  16.2 us
    all_to_all x1, blocking collectives, local(): lax.all_to_all(found, 'col', split_axis=0, concat_axis=0, tiled=True)  13.9 us
    all_to_all x1, starting transfers between devices, local(): lax.all_to_all(partial, 'col', split_axis=0, concat_axis=0, tiled=True)  9.4 us
    all_gather x1, blocking collectives, local(): potentials = lax.all_gather(mine, 'row', axis=0, tiled=False)  7.57 us
    ppermute x3, starting transfers between devices, local(): got = lax.ppermute(held, ALL, step)  7.32 us
    unnamed x19, local copies, waits for them, and re-layouts  7 us
  transfers between devices with their start and end apart: 8, of which 2 were waited for; matrix products, arithmetic and copies ran while one was open for 4% of the time, Pallas kernels for 20%

profile of v1, /device:TPU:0, one launch (start us, length us, event | category | flops | bytes accessed | tf_op | source)
XLA Modules:
  0.0 156.4 jit_solution(18392473860092954748)
XLA Ops:
  0.6 0.9 copy-done.1
  1.8 3.1 %collective-permute-start = (s32[256,128]{1,0:T(8,128)S(1)}, s32[256,128]{1,0:T(8,128)S(1)}, u32[]{:S(2)}, u32[]{:S(2)}) collective-permute-start(s32[256,128]{1,0:T(8,128)S(1)} %pack.1), channel_id=1, source_target_pairs={{0,2},{1,3},{2,0},{3,1},{4,6},{5,7},{6,4},{7,5},{8,24},{9,25},{10,... | collective-permute-start | bytes 393224 | tf_op jit(solution)/shard_map/ppermute | solution.py:523
  4.9 0.8 copy.15.owner_ref
  5.7 0.8 copy.16.slot_ref
  6.5 0.9 copy-done.2
  7.5 1.2 lists.1
  8.7 0.7 add_bitcast_fusion
  9.5 2.7 %collective-permute-start.1 = (s32[512,128]{1,0:T(8,128)S(1)}, s32[512,128]{1,0:T(8,128)S(1)}, u32[]{:S(2)}, u32[]{:S(2)}) collective-permute-start(s32[512,128]{1,0:T(8,128)S(1)} %pad_add_fusion.2), channel_id=1, source_target_pairs={{0,4},{1,5},{2,6},{3,7},{4,0},{5,1},{6,2},{7,3},{8,10},{9,11},{10,... | collective-permute-start | bytes 786440 | tf_op jit(solution)/shard_map/ppermute | solution.py:523
  12.2 0.7 copy-done.3
  12.9 7.6 %past.4.start_ref = f32[1024,256]{1,0:T(8,128)S(1)} custom-call(s32[4,64]{1,0:T(4,128)S(1)} %copy-done.3, bf16[1024,16384]{1,0:T(8,128)(2,1)} %refs_11_.1, bf16[4,16384,256]{2,1,0:T(8,128)(2,1)} %refs_10_.1, f32[1024,256]{1,0:T(8,128)S(1)} %broadcast_in_dim.8.start_ref), custom_call_target="tpu_custom_call" | custom-call | flops 2147483648 | bytes 18874368 | tf_op jit(solution)/shard_map/past/pallas_call | solution.py:205
  20.7 1.6 %collective-permute-start.2 = (s32[1024,128]{1,0:T(8,128)S(1)}, s32[1024,128]{1,0:T(8,128)S(1)}, u32[]{:S(2)}, u32[]{:S(2)}) collective-permute-start(s32[1024,128]{1,0:T(8,128)S(1)} %pad_add_fusion.1), channel_id=1, source_target_pairs={{0,1},{1,0},{2,3},{3,2},{4,5},{5,4},{6,7},{7,6},{8,12},{9,13},{10,... | collective-permute-start | bytes 1572872 | tf_op jit(solution)/shard_map/ppermute | solution.py:523
  22.3 0.7 broadcast_in_dim.21
  23.0 2.8 %all-to-all-start = ((s32[32,16,128]{2,1,0:T(8,128)}), s32[32,16,128]{2,1,0:T(8,128)S(1)}, u32[]{:S(2)}, u32[]{:S(2)}) async-start(s32[32,16,128]{2,1,0:T(8,128)} %bitcast.1), calls=%async_computation | async-start | bytes 524288 | tf_op jit(solution)/shard_map/all_to_all | solution.py:491
  25.8 7.7 %past.5.start_ref = f32[1024,256]{1,0:T(8,128)S(1)} custom-call(s32[4,64]{1,0:T(4,128)S(1)} %copy-done.4, bf16[1024,16384]{1,0:T(8,128)(2,1)} %refs_11_.1, bf16[4,16384,256]{2,1,0:T(8,128)(2,1)} %refs_10_.1, f32[1024,256]{1,0:T(8,128)S(1)} %past.4.start_ref), custom_call_target="tpu_custom_call" | custom-call | flops 2147483648 | bytes 18874368 | tf_op jit(solution)/shard_map/past/pallas_call | solution.py:205
  33.5 6.6 %all-to-all-done = s32[32,16,128]{2,1,0:T(8,128)S(1)} async-done(((s32[32,16,128]{2,1,0:T(8,128)}), s32[32,16,128]{2,1,0:T(8,128)S(1)}, u32[]{:S(2)}, u32[]{:S(2)}) %all-to-all-start) | async-done | bytes 262176 | tf_op jit(solution)/shard_map/all_to_all | solution.py:491
  40.2 1.6 collective-permute-start.3
  41.7 7.6 %past.6.start_ref = f32[1024,256]{1,0:T(8,128)S(1)} custom-call(s32[4,64]{1,0:T(4,128)S(1)} %copy-done.4, bf16[1024,16384]{1,0:T(8,128)(2,1)} %refs_11_.1, bf16[4,16384,256]{2,1,0:T(8,128)(2,1)} %refs_10_.1, f32[1024,256]{1,0:T(8,128)S(1)} %past.5.start_ref), custom_call_target="tpu_custom_call" | custom-call | flops 2147483648 | bytes 18874368 | tf_op jit(solution)/shard_map/past/pallas_call | solution.py:205
  49.4 7.6 %past.7.refs_5_ = f32[1024,256]{1,0:T(8,128)S(1)} custom-call(s32[4,64]{1,0:T(4,128)S(1)} %copy-done.4, bf16[1024,16384]{1,0:T(8,128)(2,1)} %refs_11_.1, bf16[4,16384,256]{2,1,0:T(8,128)(2,1)} %refs_10_.1, f32[1024,256]{1,0:T(8,128)S(1)} %past.6.start_ref), custom_call_target="tpu_custom_call" | custom-call | flops 2147483648 | bytes 18874368 | tf_op jit(solution)/shard_map/past/pallas_call | solution.py:205
  57.0 1.0 copy-done
  58.0 0.5 collective-permute-start.5
  58.5 1.2 fusion.refs_1_
  59.7 1.3 dynamic-slice_reduce_fusion.refs_2_
  61.0 1.0 copy-done.7
  62.0 37.9 %now.1 = (bf16[16384,256]{1,0:T(8,128)(2,1)}, s32[8,16,1280]{2,1,0:T(8,128)}) custom-call(s32[65536]{0:T(1024)} %bitcast.25, s32[32]{0:T(128)} %fusion.refs_1_, s32[32]{0:T(128)} %dynamic-slice_reduce_fusion.refs_2_, f32[512]{0:T(512)} %constant.30.clone.refs_3_, s32[4,64]{1,0:T(4,128)} %refs_4_.1, f32[1024,256]{1,0:T(8,128)} %copy-done, ...), custom_call_target="tpu_custom_call" | custom-call | flops 1073741824 | bytes 83886080 | tf_op jit(solution)/shard_map/now/pallas_call | solution.py:378
  99.9 9.4 %all-to-all-start.1 = ((s32[8,16,1280]{2,1,0:T(8,128)}), s32[8,16,1280]{2,1,0:T(8,128)S(1)}, u32[]{:S(2)}, u32[]{:S(2)}) async-start(s32[8,16,1280]{2,1,0:T(8,128)} %get-tuple-element.51), calls=%async_computation.1 | async-start | bytes 1310720 | tf_op jit(solution)/shard_map/all_to_all | solution.py:564
  109.3 0.8 constant_dynamic-slice_fusion
  110.1 16.2 %all-to-all-done.1.got_ref = s32[8,16,1280]{2,1,0:T(8,128)S(1)} async-done(((s32[8,16,1280]{2,1,0:T(8,128)}), s32[8,16,1280]{2,1,0:T(8,128)S(1)}, u32[]{:S(2)}, u32[]{:S(2)}) %all-to-all-start.1) | async-done | bytes 655392 | tf_op jit(solution)/shard_map/all_to_all | solution.py:564
  126.3 2.1 %sum.1 = f32[32,1024]{1,0:T(8,128)S(1)} custom-call(s32[8,16,1280]{2,1,0:T(8,128)S(1)} %all-to-all-done.1.got_ref), custom_call_target="tpu_custom_call" | custom-call | tf_op jit(solution)/shard_map/sum/pallas_call | solution.py:432
  128.4 7.6 %all-gather = f32[128,1024]{1,0:T(8,128)S(1)} all-gather(f32[32,1024]{1,0:T(8,128)S(1)} %sum.1), channel_id=2, replica_groups=mesh['row'=4,'col'=8] {'row'}, dimensions={0}, use_global_device_ids=true | all-gather | bytes 655360 | tf_op jit(solution)/shard_map/all_gather | solution.py:566
  136.0 5.5 %drops.1 = f32[32,2048]{1,0:T(8,128)S(1)} custom-call(s32[2,2048]{1,0:T(2,128)S(1)} %bitcast.24, f32[4,32,1024]{2,1,0:T(8,128)S(1)} %bitcast.22), custom_call_target="tpu_custom_call" | custom-call | tf_op jit(solution)/shard_map/drops/pallas_call | solution.py:468
  141.6 13.9 %all_to_all.22 = f32[8,32,256]{2,1,0:T(8,128)S(1)} all-to-all(f32[8,32,256]{2,1,0:T(8,128)S(1)} %bitcast.26), channel_id=1, replica_groups=mesh['row'=4,'col'=8] {'col'}, dimensions={0} | all-to-all | bytes 524288 | tf_op jit(solution)/shard_map/all_to_all | solution.py:570
  155.5 0.8 copy.18
  (33 shorter events, 0.7 us)
Async XLA Ops:
  0.6 1.0 copy-start.1
  1.8 7.7 %collective-permute-start = (s32[256,128]{1,0:T(8,128)S(1)}, s32[256,128]{1,0:T(8,128)S(1)}, u32[]{:S(2)}, u32[]{:S(2)}) collective-permute-start(s32[256,128]{1,0:T(8,128)S(1)} %pack.1), channel_id=1, source_target_pairs={{0,2},{1,3},{2,0},{3,1},{4,6},{5,7},{6,4},{7,5},{8,24},{9,25},{10,... | collective-permute-start | bytes 393224 | tf_op jit(solution)/shard_map/ppermute | solution.py:523
  6.5 1.0 copy-start.2
  9.5 11.1 %collective-permute-start.1 = (s32[512,128]{1,0:T(8,128)S(1)}, s32[512,128]{1,0:T(8,128)S(1)}, u32[]{:S(2)}, u32[]{:S(2)}) collective-permute-start(s32[512,128]{1,0:T(8,128)S(1)} %pad_add_fusion.2), channel_id=1, source_target_pairs={{0,4},{1,5},{2,6},{3,7},{4,0},{5,1},{6,2},{7,3},{8,10},{9,11},{10,... | collective-permute-start | bytes 786440 | tf_op jit(solution)/shard_map/ppermute | solution.py:523
  12.2 0.7 copy-start.3
  12.9 12.9 %copy-start.4 = (s32[4,64]{1,0:T(4,128)S(1)}, s32[4,64]{1,0:T(4,128)}, u32[]{:S(2)}) copy-start(s32[4,64]{1,0:T(4,128)} %refs_4_.1) | copy-start | bytes 3076
  20.7 19.4 %collective-permute-start.2 = (s32[1024,128]{1,0:T(8,128)S(1)}, s32[1024,128]{1,0:T(8,128)S(1)}, u32[]{:S(2)}, u32[]{:S(2)}) collective-permute-start(s32[1024,128]{1,0:T(8,128)S(1)} %pad_add_fusion.1), channel_id=1, source_target_pairs={{0,1},{1,0},{2,3},{3,2},{4,5},{5,4},{6,7},{7,6},{8,12},{9,13},{10,... | collective-permute-start | bytes 1572872 | tf_op jit(solution)/shard_map/ppermute | solution.py:523
  23.0 17.1 %all-to-all-start = ((s32[32,16,128]{2,1,0:T(8,128)}), s32[32,16,128]{2,1,0:T(8,128)S(1)}, u32[]{:S(2)}, u32[]{:S(2)}) async-start(s32[32,16,128]{2,1,0:T(8,128)} %bitcast.1), calls=%async_computation | async-start | bytes 524288 | tf_op jit(solution)/shard_map/all_to_all | solution.py:491
  40.1 19.6 %copy-start.6 = (s32[32,16,128]{2,1,0:T(8,128)}, s32[32,16,128]{2,1,0:T(8,128)S(1)}, u32[]{:S(2)}) copy-start(s32[32,16,128]{2,1,0:T(8,128)S(1)} %all-to-all-done) | copy-start | bytes 786436
  40.2 9.2 %copy-start.5 = (s32[2048,128]{1,0:T(8,128)}, s32[2048,128]{1,0:T(8,128)S(1)}, u32[]{:S(2)}) copy-start(s32[2048,128]{1,0:T(8,128)S(1)} %pad_add_fusion.refs_6_) | copy-start | bytes 3145732
  40.2 17.8 %collective-permute-start.3 = (s32[2048,128]{1,0:T(8,128)S(1)}, s32[2048,128]{1,0:T(8,128)}, u32[]{:S(2)}, u32[]{:S(2)}) collective-permute-start(s32[2048,128]{1,0:T(8,128)S(1)} %pad_add_fusion.refs_6_), channel_id=1, source_target_pairs={{0,16},{1,17},{2,18},{3,19},{4,20},{5,21},{6,22},{7,23},{8,9},{9,8... | collective-permute-start | bytes 3145736 | tf_op jit(solution)/shard_map/ppermute | solution.py:539
  41.7 19.3 %collective-permute-start.4 = (s32[2048,128]{1,0:T(8,128)S(1)}, s32[2048,128]{1,0:T(8,128)}, u32[]{:S(2)}, u32[]{:S(2)}) collective-permute-start(s32[2048,128]{1,0:T(8,128)S(1)} %pad_add_fusion.refs_6_), channel_id=1, source_target_pairs={{0,8},{1,9},{2,10},{3,11},{4,12},{5,13},{6,14},{7,15},{8,0},{9,1},... | collective-permute-start | bytes 3145736 | tf_op jit(solution)/shard_map/ppermute | solution.py:540
  57.0 1.0 copy-start
  58.0 3.0 %collective-permute-start.5 = (s32[2048,128]{1,0:T(8,128)}, s32[2048,128]{1,0:T(8,128)S(1)}, u32[]{:S(2)}, u32[]{:S(2)}) collective-permute-start(s32[2048,128]{1,0:T(8,128)} %collective-permute-done.3.refs_7_), channel_id=1, source_target_pairs={{0,8},{1,9},{2,10},{3,11},{4,12},{5,13},{6,14},{7,15},{8,0},{9,1},... | collective-permute-start | bytes 3145736 | tf_op jit(solution)/shard_map/ppermute | solution.py:545
  61.0 1.0 copy-start.7
  99.9 26.4 %all-to-all-start.1 = ((s32[8,16,1280]{2,1,0:T(8,128)}), s32[8,16,1280]{2,1,0:T(8,128)S(1)}, u32[]{:S(2)}, u32[]{:S(2)}) async-start(s32[8,16,1280]{2,1,0:T(8,128)} %get-tuple-element.51), calls=%async_computation.1 | async-start | bytes 1310720 | tf_op jit(solution)/shard_map/all_to_all | solution.py:564

commit v2 on v1

v2 whole, which is shorter than its diff:
```python
import functools

import jax
import jax.numpy as jnp
import numpy as np
from jax import lax
from jax.experimental import pallas as pl
from jax.experimental.pallas import tpu as pltpu
from jax.sharding import PartitionSpec as P

F32, BF16, I32 = jnp.float32, jnp.bfloat16, jnp.int32
ALL = ("row", "col")
CHAINS = 4
UNROLL = 4
GROUP = 4
LANES = 128
FULL = 32767.0
LOW = 107
PAD = 4
MEAN = float(1 << 30)


def log2(n):
    bits = int(n).bit_length() - 1
    assert 1 << bits == n
    return bits


def powers(shape=(1, LANES), exponent=None):
    if exponent is None:
        exponent = lax.broadcasted_iota(I32, shape, 1 if shape[1] == LANES else 0)
    up = jnp.full(exponent.shape, 2.0**-LOW, F32)
    down = jnp.full(exponent.shape, 2.0**LOW, F32)
    for bit in range(log2(LANES)):
        on = lax.bitwise_and(exponent, 1 << bit) > 0
        up = jnp.where(on, up * 2.0 ** (1 << bit), up)
        down = jnp.where(on, down * 2.0 ** -(1 << bit), down)
    return up, down


def scale_of(values, axis=1):
    up, down = powers((1, LANES) if axis == 1 else (LANES, 1))
    most = jnp.max(jnp.abs(values), axis=axis, keepdims=True)
    fits = up >= most
    inverse = jnp.max(jnp.where(fits, down, 0.0), axis=axis, keepdims=True)
    index = jnp.sum(jnp.where(fits, 0, 1), axis=axis, keepdims=True)
    return index, inverse


def coded(values, inverse):
    return jnp.floor(values * (inverse * FULL) + 0.5).astype(I32)


def pair(low, high):
    return lax.bitwise_or(lax.shift_left(high, 16), lax.bitwise_and(low, 0xFFFF))


def low_of(words):
    return lax.shift_right_arithmetic(lax.shift_left(words, 16), 16)


def high_of(words):
    return lax.shift_right_arithmetic(words, 16)


def vmem(n=1):
    return [pl.BlockSpec(memory_space=pltpu.VMEM)] * n


def params(mib, **more):
    return pltpu.CompilerParams(vmem_limit_bytes=mib << 20, **more)


def pack_kernel(current_ref, out_ref, index_ref):
    values = current_ref[...]
    index, inverse = scale_of(values, axis=0)
    codes = coded(values, inverse)
    half = codes.shape[1] // 2
    out_ref[...] = pair(codes[:, :half], codes[:, half:])
    index_ref[0:1, :] = index[:, :half]
    index_ref[1:2, :] = index[:, half:]


def pack(currents):
    rows, scenarios = currents.shape
    return pl.pallas_call(
        pack_kernel,
        out_shape=(
            jax.ShapeDtypeStruct((rows, scenarios // 2), I32),
            jax.ShapeDtypeStruct((2, scenarios // 2), I32),
        ),
        in_specs=vmem(1),
        out_specs=tuple(vmem(2)),
        compiler_params=params(16),
        name="pack",
    )(currents)


def node_bits(chain_rows):
    return log2(chain_rows) + 2


def list_kernel(sizes, owner_ref, slot_ref, out_ref, tally_ref):
    rows_of, owned, block, capacity, chain_rows = sizes
    count = owner_ref.shape[1]
    ends = 2 * count
    owner = jnp.concatenate([owner_ref[0:1, :], owner_ref[1:2, :]], axis=1)
    slot = jnp.concatenate([slot_ref[0:1, :], slot_ref[1:2, :]], axis=1)
    end = lax.broadcasted_iota(I32, (1, ends), 1)
    branch = lax.bitwise_and(end, count - 1)
    column = lax.shift_right_logical(owner, log2(rows_of))
    node = lax.bitwise_and(owner, rows_of - 1) * owned + slot
    at_block = lax.shift_right_logical(node, log2(block))
    chain = lax.bitwise_and(at_block, CHAINS - 1)
    place = lax.shift_right_logical(at_block, log2(CHAINS)) * block
    place = place + lax.bitwise_and(node, block - 1)
    row = jnp.where(end >= count, 0, count) + branch
    entry = 2 * (place + PAD) + lax.shift_left(2 * row, node_bits(chain_rows))
    key = column * CHAINS + chain
    hit = key == lax.broadcasted_iota(I32, (LANES, ends), 0)
    onehot = jnp.where(hit, 1.0, 0.0).astype(BF16)
    before = lax.broadcasted_iota(I32, (ends, ends), 0) < lax.broadcasted_iota(I32, (ends, ends), 1)
    before = jnp.where(before, 1.0, 0.0).astype(BF16)
    ranks = jnp.dot(onehot, before, preferred_element_type=F32)
    rank = jnp.sum(jnp.where(hit, ranks, 0.0), axis=0, keepdims=True).astype(I32)
    placed = rank == lax.broadcasted_iota(I32, (capacity, ends), 0)
    contract = (((1,), (1,)), ((), ()))
    total = jnp.zeros((LANES, capacity), I32)
    for piece in range(-(-(node_bits(chain_rows) + log2(count) + 2) // 8)):
        part = lax.bitwise_and(lax.shift_right_logical(entry, 8 * piece), 255)
        part = jnp.where(placed, part.astype(F32), 0.0).astype(BF16)
        found = lax.dot_general(onehot, part, contract, preferred_element_type=F32)
        total = total + lax.shift_left(found.astype(I32), 8 * piece)
    ones = jnp.ones((8, ends), BF16)
    tally = lax.dot_general(ones, onehot, contract, preferred_element_type=F32)
    tally_ref[...] = tally[0:1].astype(I32)
    out_ref[...] = total[: out_ref.shape[0]]


def make_lists(owner, slot, sizes, keys):
    return pl.pallas_call(
        functools.partial(list_kernel, sizes),
        out_shape=(jax.ShapeDtypeStruct((keys, sizes[3]), I32), jax.ShapeDtypeStruct((1, LANES), I32)),
        in_specs=vmem(2),
        out_specs=tuple(vmem(2)),
        compiler_params=params(24),
        name="lists",
    )(owner.T, slot.T)


def routes(row_count, col_count):
    col_bits, row_bits = log2(col_count), log2(row_count)
    across = [1 << b for b in (*range(1, col_bits), *([0] if col_bits else []))]
    along = [1 << (b + col_bits) for b in range(1, row_bits)]
    return (across + along, along + across), 1 << col_bits


def masks(steps):
    found = [0]
    for step in steps:
        found = found + [m ^ step for m in found]
    return found


def sources(row_count, col_count):
    orders, core = routes(row_count, col_count)
    devices = row_count * col_count
    table = np.zeros((devices, 2, 2, devices // 4), np.int32)
    for me in range(devices):
        for far, holder in enumerate((me, me ^ core)):
            found = [holder ^ mask for mask in masks(orders[1 if holder & core else 0])]
            table[me, :, far] = np.reshape(found, (2, devices // 4))
    return table.reshape(devices, devices)


def gather_steps(row_count, col_count):
    orders, core = routes(row_count, col_count)
    devices = row_count * col_count
    pairs = []
    for first, second in zip(*orders):
        pairs.append([(d, d ^ (second if d & core else first)) for d in range(devices)])
    sibling = [(d, d ^ core) for d in range(devices)]
    return pairs, sibling


def past_kernel(block, slots, part, parts, todo_ref, owner_ref, start_ref, history_ref, coef_ref, out_ref, coef, source_of, sems):
    count = owner_ref[owner_ref.shape[0] - 1]
    first, last = count * part // parts, count * (part + 1) // parts

    def copies(t):
        slot = lax.rem(t, slots)
        i = owner_ref[t]
        for g in range(GROUP):
            entry = jnp.maximum(todo_ref[t * GROUP + g], 0)
            k = lax.shift_right_logical(entry, 3)
            rows = pl.ds(pl.multiple_of(k * block, block), block)
            yield pltpu.make_async_copy(
                coef_ref.at[pl.ds(pl.multiple_of(i * block, block), block), rows],
                coef.at[slot, :, pl.ds(g * block, block)],
                sems.at[slot, 0, g],
            )
            yield pltpu.make_async_copy(
                history_ref.at[lax.bitwise_and(entry, 7), rows],
                source_of.at[slot, pl.ds(g * block, block)],
                sems.at[slot, 1, g],
            )

    @pl.loop(first, jnp.minimum(first + slots - 1, last))
    def _(t):
        for copy in copies(t):
            copy.start()

    out_ref[...] = start_ref[...]

    @pl.loop(first, last)
    def _(t):
        @pl.when(t + slots - 1 < last)
        def _():
            for copy in copies(t + slots - 1):
                copy.start()

        for copy in copies(t):
            copy.wait()
        slot = lax.rem(t, slots)
        for g in range(1, GROUP):
            @pl.when(todo_ref[t * GROUP + g] < 0)
            def _():
                source_of[slot, g * block : (g + 1) * block, :] = jnp.zeros((block, source_of.shape[2]), BF16)

        out_ref[owner_ref[t]] += jnp.dot(coef[slot], source_of[slot], preferred_element_type=F32)


def past_product(todo, owner, coefficients, history, start, block, part, parts):
    row_blocks, _, scenarios = start.shape
    slots = 6
    moved = (coefficients.size + history.size // history.shape[0] * row_blocks) * 2 // parts
    smem = pl.BlockSpec(memory_space=pltpu.SMEM)
    hbm = pl.BlockSpec(memory_space=pl.ANY)
    return pl.pallas_call(
        functools.partial(past_kernel, block, slots, part, parts),
        out_shape=jax.ShapeDtypeStruct(start.shape, F32),
        in_specs=[smem, smem, *vmem(1), hbm, hbm],
        out_specs=vmem()[0],
        scratch_shapes=[
            pltpu.VMEM((slots, block, GROUP * block), BF16),
            pltpu.VMEM((slots, GROUP * block, scenarios), BF16),
            pltpu.SemaphoreType.DMA((slots, 2, GROUP)),
        ],
        compiler_params=params(32),
        cost_estimate=pl.CostEstimate(
            flops=2 * coefficients.size * scenarios // parts, bytes_accessed=moved, transcendentals=0
        ),
        name="past",
    )(todo, owner, start, history, coefficients)


def scan_kernel(delays_ref, now_ref, now_owner_ref, past_ref, past_owner_ref):
    row_blocks, col_blocks = delays_ref.shape
    found = (jnp.int32(0), jnp.int32(0))
    lists, owners = (now_ref, past_ref), (now_owner_ref, past_owner_ref)
    for i in range(row_blocks):
        first = [at // GROUP for at in found]

        def look(k, at, i=i):
            now, past = at
            for g in range(GROUP):
                delay = delays_ref[i, k * GROUP + g]
                here = jnp.where(delay == 0, 1, 0)
                now_ref[now] = k * GROUP + g
                past_ref[past] = (k * GROUP + g) * 8 + delay - 1
                now, past = now + here, past + (1 - here)
            return now, past

        found = lax.fori_loop(0, col_blocks // GROUP, look, found)
        for g in range(GROUP):
            now_ref[found[0] + g] = -1
            past_ref[found[1] + g] = -1
        found = tuple((at + (GROUP - 1)) // GROUP * GROUP for at in found)
        for n in range(2):
            @pl.loop(first[n], found[n] // GROUP)
            def _(t):
                owners[n][t] = i

    for n in range(2):
        owners[n][owners[n].shape[0] - 1] = found[n] // GROUP


def scan(delays):
    row_blocks, col_blocks = delays.shape
    groups = row_blocks * (col_blocks // GROUP + 1)
    smem = pl.BlockSpec(memory_space=pltpu.SMEM)
    one = (jax.ShapeDtypeStruct((groups * GROUP,), I32), jax.ShapeDtypeStruct((groups + 1,), I32))
    return pl.pallas_call(
        scan_kernel,
        out_shape=one + one,
        in_specs=[smem],
        out_specs=(smem,) * 4,
        name="scan",
    )(delays)


def row_copies(pieces, rows, sems):
    part = pieces[0].shape[0]
    return [
        pltpu.make_async_copy(piece, rows.at[pl.ds(n * part, part)], sems.at[n]) for n, piece in enumerate(pieces)
    ]


def decode(index_ref, order_ref, first, blocks, branch_rows, skip, codes, rows):
    @pl.loop(0, blocks)
    def _(place):
        scales, _ = powers(exponent=index_ref[order_ref[first + place]])
        scales = scales * (1.0 / FULL)
        words = codes[pl.ds(pl.multiple_of((skip + place) * branch_rows, branch_rows), branch_rows), :]
        base = place * (4 * branch_rows)
        for side, part in enumerate((low_of(words), high_of(words))):
            value = part.astype(F32) * scales[side : side + 1, :]
            rows[pl.ds(base + side, branch_rows, stride=2), :] = value
            rows[pl.ds(base + 2 * branch_rows + side, branch_rows, stride=2), :] = -value


def scatter(sizes, first, blocks, lists_ref, order_ref, tally_ref, rows, acc):
    capacity, words, branch_rows = sizes
    bits = node_bits(acc[0].shape[0] // 2 - PAD)

    @pl.loop(0, blocks)
    def _(place):
        source = order_ref[first + place]
        base = place * (4 * branch_rows)
        start = source * words

        @pl.loop(0, (tally_ref[source] + (UNROLL - 1)) // UNROLL)
        def _(j):
            for u in range(UNROLL):
                after = []
                for chain in range(CHAINS):
                    entry = lists_ref[start + chain * capacity + j * UNROLL + u]
                    row = pl.multiple_of(base + lax.shift_right_logical(entry, bits), 2)
                    at = pl.ds(pl.multiple_of(lax.bitwise_and(entry, (1 << bits) - 1), 2), 2)
                    after.append((acc[chain], at, acc[chain][at, :] + rows[pl.ds(row, 2), :]))
                for part, at, value in after:
                    part[at, :] = value


def add_ends(sizes, first, lists_ref, order_ref, tally_ref, index_ref, codes, rows, acc):
    branch_rows = sizes[2]
    blocks = codes.shape[0] // branch_rows
    batch = rows.shape[0] // (4 * branch_rows)
    for skip in range(0, blocks, batch):
        decode(index_ref, order_ref, first + skip, batch, branch_rows, skip, codes, rows)
        scatter(sizes, first + skip, batch, lists_ref, order_ref, tally_ref, rows, acc)


def early_kernel(sizes, lists_ref, order_ref, tally_ref, index_ref, one_ref, two_ref, *more):
    acc, (codes, rows, sems) = more[:CHAINS], more[CHAINS:]
    copies = row_copies((one_ref, two_ref), codes, sems)
    for copy in copies:
        copy.start()
    clear = 512
    for part in acc:
        part[0 : 2 * PAD, :] = jnp.zeros((2 * PAD, LANES), F32)

        @pl.loop(0, part.shape[0] // clear)
        def _(n):
            part[pl.ds(pl.multiple_of(n * clear + 2 * PAD, 8), clear), :] = jnp.zeros((clear, LANES), F32)
    for copy in copies:
        copy.wait()
    add_ends(sizes, 0, lists_ref, order_ref, tally_ref, index_ref, codes, rows, acc)


def early_scatter(lists, order, tally, index, pieces, nodes, sizes):
    smem = pl.BlockSpec(memory_space=pltpu.SMEM)
    hbm = pl.BlockSpec(memory_space=pl.ANY)
    return pl.pallas_call(
        functools.partial(early_kernel, sizes),
        out_shape=tuple(pltpu.VMEM((2 * (nodes // CHAINS + PAD), LANES), F32) for _ in range(CHAINS)),
        in_specs=[smem] * 3 + vmem(1) + [hbm] * 2,
        out_specs=tuple(vmem(CHAINS)),
        scratch_shapes=[
            pltpu.VMEM((2 * pieces[0].shape[0], pieces[0].shape[1]), I32),
            pltpu.VMEM((4 * min(2 * pieces[0].shape[0], 16 * sizes[2]), LANES), F32),
            pltpu.SemaphoreType.DMA((2,)),
        ],
        compiler_params=params(38),
        cost_estimate=pl.CostEstimate(flops=1 << 28, bytes_accessed=32 << 20, transcendentals=0),
        name="early",
    )(lists, order, tally, index, *pieces)


def now_kernel(
    block, slots, chunks, sizes,
    lists_ref, order_ref, tally_ref, todo_ref, owner_ref, past_ref, index_ref,
    one_ref, two_ref, history_ref, coef_ref,
    charge_ref, out_ref, acc,
    codes, rows, charge, coef, source_of, total, row_sem, load_sem, store_sem, coef_sem,
):
    row_blocks, col_blocks = total.shape[0], charge.shape[0] // block
    copies = row_copies((one_ref, two_ref), codes, row_sem)
    for copy in copies:
        copy.start()
    load = pltpu.make_async_copy(history_ref.at[0], charge, load_sem)
    load.start()

    count = owner_ref[owner_ref.shape[0] - 1]

    def coef_copy(t, g):
        i = owner_ref[t]
        k = jnp.maximum(todo_ref[t * GROUP + g], 0)
        slot = lax.rem(t, slots)
        return pltpu.make_async_copy(
            coef_ref.at[pl.ds(pl.multiple_of(i * block, block), block),
                        pl.ds(pl.multiple_of(k * block, block), block)],
            coef.at[slot, :, pl.ds(g * block, block)],
            coef_sem.at[slot, g],
        )

    @pl.loop(0, jnp.minimum(count, slots))
    def _(t):
        for g in range(GROUP):
            coef_copy(t, g).start()

    for copy in copies:
        copy.wait()
    add_ends(sizes, order_ref.shape[0] // 2, lists_ref, order_ref, tally_ref, index_ref, codes, rows, acc)
    load.wait()

    def store(k):
        at = pl.ds(pl.multiple_of(k * block, block), block)
        return pltpu.make_async_copy(charge.at[at], charge_ref.at[at], store_sem)

    @pl.loop(0, col_blocks // CHAINS)
    def _(group):
        for chain in range(CHAINS):
            k = group * CHAINS + chain
            at = pl.ds(pl.multiple_of(k * block, block), block)
            for side in range(2):
                lanes = slice(side * LANES, (side + 1) * LANES)
                held = pl.ds(group * (2 * block) + (2 * PAD + side), block, stride=2)
                charge[at, lanes] = (charge[at, lanes].astype(F32) + acc[chain][held, :]).astype(BF16)
            store(k).start()

    for i in range(row_blocks):
        total[i] = past_ref[i]

    @pl.loop(0, count)
    def _(t):
        for g in range(GROUP):
            k = todo_ref[t * GROUP + g]
            held = charge[pl.ds(pl.multiple_of(jnp.maximum(k, 0) * block, block), block), :]
            source_of[g * block : (g + 1) * block, :] = jnp.where(k >= 0, held, jnp.zeros_like(held))
        for g in range(GROUP):
            coef_copy(t, g).wait()
        slot = lax.rem(t, slots)
        total[owner_ref[t]] += jnp.dot(coef[slot], source_of[...], preferred_element_type=F32)

        @pl.when(t + slots < count)
        def _():
            for g in range(GROUP):
                coef_copy(t + slots, g).start()

    turned = jnp.concatenate([total[i].T for i in range(row_blocks)], axis=1)
    nodes = turned.shape[1]
    mean = jnp.sum(turned, axis=1, keepdims=True) * (1.0 / nodes)
    rest = turned - mean
    index, inverse = scale_of(rest)
    codes = coded(rest, inverse)
    mean_index, mean_inverse = scale_of(mean)
    mean_code = jnp.floor(mean * mean_inverse * MEAN).astype(I32)
    lane = lax.broadcasted_iota(I32, (turned.shape[0], LANES), 1)
    head = jnp.where(lane == 1, mean_index, mean_code)
    head = jnp.where(lane == 0, index, head)
    chunk = turned.shape[0] // chunks
    half = chunk // 2
    for c in range(chunks):
        one = slice(c * chunk, c * chunk + half)
        two = slice(c * chunk + half, (c + 1) * chunk)
        out_ref[c, :, :nodes] = pair(codes[one], codes[two])
        out_ref[c, :, nodes:] = jnp.concatenate([head[one, : LANES // 2], head[two, : LANES // 2]], axis=1)

    pltpu.make_async_copy(charge, charge_ref, store_sem).wait()


def now_product(lists, order, tally, index, todo, owner, past, acc, pieces, history, coefficients, block, chunks, sizes):
    row_blocks, _, scenarios = past.shape
    rows = row_blocks * block
    nodes = history.shape[1]
    slots = 8
    smem = pl.BlockSpec(memory_space=pltpu.SMEM)
    hbm = pl.BlockSpec(memory_space=pl.ANY)
    held = [pltpu.with_memory_space_constraint(part, pltpu.VMEM) for part in acc]
    before, count = 11, len(acc)

    def kernel(*refs):
        sums = refs[before + count + 2 : before + 2 * count + 2]
        ins, outs = refs[:before], refs[before + count : before + count + 2]
        now_kernel(block, slots, chunks, sizes, *ins, *outs, sums, *refs[before + 2 * count + 2 :])

    return pl.pallas_call(
        kernel,
        out_shape=(
            jax.ShapeDtypeStruct((nodes, scenarios), BF16),
            jax.ShapeDtypeStruct((chunks, scenarios // chunks // 2, rows + LANES), I32),
            *[pltpu.VMEM(part.shape, F32) for part in acc],
        ),
        in_specs=[smem] * 5 + vmem(2) + [hbm] * 4 + vmem(count),
        out_specs=(hbm, *vmem(1 + count)),
        input_output_aliases={before + n: 2 + n for n in range(count)},
        scratch_shapes=[
            pltpu.VMEM((2 * pieces[0].shape[0], scenarios // 2), I32),
            pltpu.VMEM((4 * min(2 * pieces[0].shape[0], 16 * sizes[2]), LANES), F32),
            pltpu.VMEM((nodes, scenarios), BF16),
            pltpu.VMEM((slots, block, GROUP * block), BF16),
            pltpu.VMEM((GROUP * block, scenarios), BF16),
            pltpu.VMEM((row_blocks, block, scenarios), F32),
            pltpu.SemaphoreType.DMA((2,)),
            pltpu.SemaphoreType.DMA,
            pltpu.SemaphoreType.DMA,
            pltpu.SemaphoreType.DMA((slots, GROUP)),
        ],
        compiler_params=params(40),
        cost_estimate=pl.CostEstimate(flops=1 << 30, bytes_accessed=80 << 20, transcendentals=0),
        name="now",
    )(lists, order, tally, todo, owner, past, index, *pieces, history, coefficients, *held)[:2]


def sum_kernel(got_ref, out_ref):
    sources, half, width = got_ref.shape
    nodes = width - LANES
    up, _ = powers()
    lane = lax.broadcasted_iota(I32, (half, LANES), 1)

    def power(index):
        return jnp.sum(jnp.where(lane == index, up, 0.0), axis=1, keepdims=True)

    for side in range(2):
        total = jnp.zeros((half, nodes), F32)
        for source in range(sources):
            words = got_ref[source, :, :nodes]
            head = got_ref[source, :, nodes:]
            at = side * (LANES // 2)
            codes = (high_of(words) if side else low_of(words)).astype(F32)
            mean = head[:, at + 2 : at + 3].astype(F32) * (power(head[:, at + 1 : at + 2]) * (1.0 / MEAN))
            total = total + (codes * (power(head[:, at : at + 1]) * (1.0 / FULL)) + mean)
        out_ref[side * half : (side + 1) * half, :] = total


def sum_columns(got):
    _, half, width = got.shape
    return pl.pallas_call(
        sum_kernel,
        out_shape=jax.ShapeDtypeStruct((2 * half, width - LANES), F32),
        in_specs=vmem(1),
        out_specs=vmem()[0],
        compiler_params=params(16),
        name="sum",
    )(got)


def drop_kernel(node_ref, potential_ref, out_ref):
    row_count, excitations, nodes = potential_ref.shape
    per_row = nodes // LANES
    groups = excitations // 8

    @pl.loop(0, node_ref.shape[1] // LANES)
    def _(group):
        at = pl.ds(pl.multiple_of(group * LANES, LANES), LANES)
        found = [[None] * groups, [None] * groups]
        for end in range(2):
            node = jnp.broadcast_to(node_ref[pl.ds(end, 1), at], (8, LANES))
            inner = lax.bitwise_and(node, LANES - 1)
            outer = lax.shift_right_logical(node, log2(LANES))
            for e in range(groups):
                value = jnp.zeros((8, LANES), F32)
                for h in range(row_count * per_row):
                    lanes = slice(h % per_row * LANES, (h % per_row + 1) * LANES)
                    held = potential_ref[h // per_row, e * 8 : (e + 1) * 8, lanes]
                    seen = jnp.take_along_axis(held, inner, axis=1, mode="promise_in_bounds")
                    value = jnp.where(outer == h, seen, value)
                found[end][e] = value
        for e in range(groups):
            out_ref[e * 8 : (e + 1) * 8, at] = found[0][e] - found[1][e]


def row_drops(nodes, potentials):
    return pl.pallas_call(
        drop_kernel,
        out_shape=jax.ShapeDtypeStruct((potentials.shape[1], nodes.shape[1]), F32),
        in_specs=vmem(2),
        out_specs=vmem()[0],
        compiler_params=params(24),
        name="drops",
    )(nodes, potentials)


def branch_lists(index, owner, slot, slab_owner, slab_offset, col_count, share, sizes):
    lists, tally = make_lists(owner, slot, sizes, col_count * CHAINS)
    slab = (slab_owner * share + slab_offset).T.reshape(-1, LANES)
    return lists.reshape(col_count, -1, LANES), tally, jnp.concatenate([index, slab], axis=0)


def share_lists(lists, tally, slab, row_count, col_count):
    common = jnp.concatenate([tally, slab], axis=0)
    extra = -(lists.shape[1] + common.shape[0]) % 8
    common = jnp.concatenate([common, jnp.zeros((extra, LANES), I32)], axis=0)
    common = jnp.broadcast_to(common[None], (col_count, *common.shape))
    message = jnp.concatenate([lists, common], axis=1)
    message = jnp.broadcast_to(message[None], (row_count, *message.shape)).reshape(-1, LANES)
    return lax.all_to_all(message, ALL, split_axis=0, concat_axis=0, tiled=True)


def local(currents, branch_owner, branch_slot, history, coefficients, delays, slab_owner, slab_offset):
    row_count = lax.axis_size("row")
    col_count = lax.axis_size("col")
    devices = row_count * col_count
    branch_rows, scenarios = currents.shape
    owned = history.shape[1] // row_count
    block = coefficients.shape[1] // delays.shape[1]
    per_owner = 8 * branch_rows // devices
    capacity = -(-min(2 * branch_rows, row_count * per_owner) // LANES) * LANES
    chain_rows = history.shape[1] // CHAINS
    share = coefficients.shape[0] * row_count // devices
    my_row, my_col = lax.axis_index("row"), lax.axis_index("col")
    me = my_row * col_count + my_col
    pairs, sibling = gather_steps(row_count, col_count)
    parts = 2
    past = jnp.zeros((delays.shape[0], block, scenarios), F32)
    together = lax.optimization_barrier

    def add_past(past, part):
        return past_product(late, late_owner, coefficients, history, past, block, part, parts)

    held, index = pack(currents)
    order = lax.dynamic_slice_in_dim(jnp.asarray(sources(row_count, col_count)), me, 1, 0)[0]
    jobs = {1: (0,), 2: (1,)}
    message = None
    for number, step in enumerate(pairs[:-1]):
        held, past = together((held, past))
        got = lax.ppermute(held, ALL, step)
        for job in jobs.get(number, ()):
            past = add_past(past, job)
        if number == 0:
            lists, tally, slab = branch_lists(
                index, branch_owner, branch_slot, slab_owner, slab_offset, col_count, share,
                (row_count, owned, block, capacity, chain_rows),
            )
            todo, owner, late, late_owner = scan(delays)
            got, past, lists, tally, slab, late = together((got, past, lists, tally, slab, late))
            message = share_lists(lists, tally, slab, row_count, col_count)
        elif number == len(pairs) - 2:
            got, past, message, order = together((got, past, message, order))
        else:
            got, past = together((got, past))
        held = jnp.concatenate([held, got], axis=0)
    held, past = together((held, past))
    mid = lax.ppermute(held, ALL, pairs[-1])
    far = lax.ppermute(held, ALL, sibling)

    list_tiles = CHAINS * capacity // LANES
    slab_rows = slab_owner.shape[0]
    slab_tiles = 2 * slab_rows // LANES
    width = message.shape[0] // devices
    message = message.reshape(devices, width, LANES)
    tally = lax.dynamic_slice_in_dim(message[:, list_tiles], my_col * CHAINS, CHAINS, 1).max(axis=1)
    row_slab = lax.dynamic_slice_in_dim(message, my_row * col_count, col_count, 0)
    row_slab = row_slab[:, list_tiles + 3 : list_tiles + 3 + slab_tiles]
    index = message[:, list_tiles + 1 : list_tiles + 3]
    row_slab = row_slab.reshape(col_count, 2, slab_rows).transpose(1, 0, 2).reshape(2, col_count * slab_rows)

    lists = message.reshape(-1)
    sizes = (capacity, width * LANES, branch_rows)
    acc = early_scatter(lists, order, tally, index, (held, far), history.shape[1], sizes)
    mid, past, acc = together((mid, past, acc))
    last = lax.ppermute(mid, ALL, sibling)
    charge, partial = now_product(
        lists, order, tally, index, todo, owner, past, acc, (mid, last), history, coefficients,
        block, col_count, sizes,
    )

    got = lax.all_to_all(partial, "col", split_axis=0, concat_axis=0, tiled=True)
    mine = sum_columns(got)
    potentials = lax.all_gather(mine, "row", axis=0, tiled=False)
    found = row_drops(row_slab, potentials)
    excitations = found.shape[0]
    found = found.reshape(excitations, col_count, slab_rows).transpose(1, 0, 2)
    found = lax.all_to_all(found, "col", split_axis=0, concat_axis=0, tiled=True)
    return charge, found.reshape(col_count * excitations, slab_rows).T


def solution(mesh):
    both = P(("row", "col"), None)
    placed = (both, both, both, P(None, "col", None), P("row", "col"), P("row", "col"), both, both)
    return jax.shard_map(
        local,
        mesh=mesh,
        in_specs=placed,
        out_specs=(P("col", None), both),
        check_vma=False,
    )
```

time: 156 us -> 141 us (0.904)
  Pallas kernels: 77.5 us -> 68.7 us
  waiting for transfers between devices: 22.8 us -> 17 us
  blocking collectives: 21.5 us -> 19.4 us
    pallas_call x1, Pallas kernels: 37.9 us -> 21.3 us  [now_product(): pl.pallas_call(kernel, out_shape=(jax.ShapeDtypeStruct((nodes, scenarios)...]
    pallas_call x5, Pallas kernels: 30.8 us -> 39.1 us  [the longest x2 24.3 us: past_product(): pl.pallas_call(functools.partial(past_kernel, block, slots, part, parts),...]
    all_to_all x1, waiting for transfers between devices: 6.58 us -> 0.01 us  [share_lists(): return lax.all_to_all(message, ALL, split_axis=0, concat_axis=0, tiled=True)]
    ppermute x1, waiting for transfers between devices: 0.01 us -> 2.56 us  [local(): last = lax.ppermute(mid, ALL, sibling)]
    all_to_all x1, waiting for transfers between devices: 16.2 us -> 14.4 us  [local(): lax.all_to_all(partial, 'col', split_axis=0, concat_axis=0, tiled=True)]
    unnamed x19 -> x28, local copies, waits for them, and re-layouts: 7 us -> 7.47 us
  transfers between devices with their start and end apart: 8 -> 8, of which waited for: 2 -> 2; matrix products, arithmetic and copies ran while one was open for 4% -> 4% of each run, Pallas kernels for 20% -> 28%
where the time goes in v2:
time: 141 us; the launch traced here: 140 us
  Pallas kernels  68.7 us (49%)
  starting transfers between devices  20.9 us (15%)
  blocking collectives  19.4 us (14%)
  waiting for transfers between devices  17 us (12%)
  local copies, waits for them, and re-layouts  11 us (8%)
  other arithmetic  2.16 us (2%)
    pallas_call x2, Pallas kernels, past_product(): pl.pallas_call(functools.partial(past_kernel, block, slots, part, parts),...  24.3 us
    pallas_call x1, Pallas kernels, now_product(): pl.pallas_call(kernel, out_shape=(jax.ShapeDtypeStruct((nodes, scenarios)...  21.3 us
    all_to_all x1, waiting for transfers between devices, local(): lax.all_to_all(partial, 'col', split_axis=0, concat_axis=0, tiled=True)  14.4 us
    all_to_all x1, blocking collectives, local(): lax.all_to_all(found, 'col', split_axis=0, concat_axis=0, tiled=True)  12.9 us
    pallas_call x1, Pallas kernels, early_scatter(): pl.pallas_call(functools.partial(early_kernel, sizes), out_shape=tuple((p...  11.4 us
    all_to_all x1, starting transfers between devices, local(): lax.all_to_all(partial, 'col', split_axis=0, concat_axis=0, tiled=True)  8.21 us
    ppermute x3, starting transfers between devices, local(): got = lax.ppermute(held, ALL, step)  7.72 us
    unnamed x28, local copies, waits for them, and re-layouts  7.47 us
  transfers between devices with their start and end apart: 8, of which 2 were waited for; matrix products, arithmetic and copies ran while one was open for 4% of the time, Pallas kernels for 28%

profile of v2, /device:TPU:0, one launch (start us, length us, event | category | flops | bytes accessed | tf_op | source)
XLA Modules:
  0.0 140.0 jit_solution(3659660202636883345)
XLA Ops:
  0.6 0.9 copy-done.1
  1.7 3.1 %collective-permute-start = (s32[256,128]{1,0:T(8,128)S(1)}, s32[256,128]{1,0:T(8,128)S(1)}, u32[]{:S(2)}, u32[]{:S(2)}) collective-permute-start(s32[256,128]{1,0:T(8,128)S(1)} %get-tuple-element.43), channel_id=1, source_target_pairs={{0,2},{1,3},{2,0},{3,1},{4,6},{5,7},{6,4},{7,5},{8,24},{9,25},{10,... | collective-permute-start | bytes 393224 | tf_op jit(solution)/shard_map/ppermute | solution.py:638
  4.8 0.7 add_bitcast_fusion
  5.5 3.3 %scan.1 = (s32[272]{0:T(512)}, s32[69]{0:T(128)}, s32[272]{0:T(512)}, s32[69]{0:T(128)}) custom-call(s32[4,64]{1,0:T(4,128)} %delays_ref.1), custom_call_target="tpu_custom_call" | custom-call | tf_op jit(solution)/shard_map/scan/pallas_call | solution.py:293
  8.8 0.7 copy-done.4
  9.5 0.7 copy-done.5
  10.9 2.7 %collective-permute-start.1 = (s32[512,128]{1,0:T(8,128)S(1)}, s32[512,128]{1,0:T(8,128)S(1)}, u32[]{:S(2)}, u32[]{:S(2)}) collective-permute-start(s32[512,128]{1,0:T(8,128)S(1)} %pad_add_fusion.2), channel_id=1, source_target_pairs={{0,4},{1,5},{2,6},{3,7},{4,0},{5,1},{6,2},{7,3},{8,10},{9,11},{10,... | collective-permute-start | bytes 786440 | tf_op jit(solution)/shard_map/ppermute | solution.py:638
  13.7 0.7 copy-done.2
  14.4 0.7 copy-done.6
  15.1 11.9 %past.2.start_ref = f32[4,256,256]{2,1,0:T(8,128)S(1)} custom-call(s32[272]{0:T(512)S(1)} %copy-done.2, s32[69]{0:T(128)S(1)} %copy-done.6, f32[4,256,256]{2,1,0:T(8,128)S(1)} %broadcast_in_dim.8.start_ref, bf16[4,16384,256]{2,1,0:T(8,128)(2,1)} %refs_9_.1, bf16[1024,16384]{1,0:T(8,128)(2,1)} %refs_10_.1), custom_call_target="tpu_custom_call" | custom-call | flops 4294967296 | bytes 33554432 | tf_op jit(solution)/shard_map/past/pallas_call | solution.py:239
  27.1 2.0 %collective-permute-start.2 = (s32[1024,128]{1,0:T(8,128)S(1)}, s32[1024,128]{1,0:T(8,128)S(1)}, u32[]{:S(2)}, u32[]{:S(2)}) collective-permute-start(s32[1024,128]{1,0:T(8,128)S(1)} %pad_add_fusion.1), channel_id=1, source_target_pairs={{0,1},{1,0},{2,3},{3,2},{4,5},{5,4},{6,7},{7,6},{8,12},{9,13},{10,... | collective-permute-start | bytes 1572872 | tf_op jit(solution)/shard_map/ppermute | solution.py:638
  29.1 0.7 broadcast_in_dim.21
  29.8 2.6 %all-to-all-start = ((s32[32,16,128]{2,1,0:T(8,128)}), s32[32,16,128]{2,1,0:T(8,128)S(1)}, u32[]{:S(2)}, u32[]{:S(2)}) async-start(s32[32,16,128]{2,1,0:T(8,128)} %bitcast.3), calls=%async_computation | async-start | bytes 524288 | tf_op jit(solution)/shard_map/all_to_all | solution.py:608
  32.4 1.2 fusion.order_ref.refs_1_
  33.6 12.4 %past.3.refs_5_ = f32[4,256,256]{2,1,0:T(8,128)S(1)} custom-call(s32[272]{0:T(512)S(1)} %copy-done.3, s32[69]{0:T(128)S(1)} %copy-done.7, f32[4,256,256]{2,1,0:T(8,128)S(1)} %past.2.start_ref, bf16[4,16384,256]{2,1,0:T(8,128)(2,1)} %refs_9_.1, bf16[1024,16384]{1,0:T(8,128)(2,1)} %refs_10_.1), custom_call_target="tpu_custom_call" | custom-call | flops 4294967296 | bytes 33554432 | tf_op jit(solution)/shard_map/past/pallas_call | solution.py:239
  46.0 1.0 copy-done
  47.1 0.7 collective-permute-start.4
  47.8 1.6 %collective-permute-start.3 = (s32[2048,128]{1,0:T(8,128)S(1)}, s32[2048,128]{1,0:T(8,128)S(1)}, u32[]{:S(2)}, u32[]{:S(2)}) collective-permute-start(s32[2048,128]{1,0:T(8,128)S(1)} %pad_add_fusion.one_ref), channel_id=1, source_target_pairs={{0,16},{1,17},{2,18},{3,19},{4,20},{5,21},{6,22},{7,23},{8,9},{9,8... | collective-permute-start | bytes 3145736 | tf_op jit(solution)/shard_map/ppermute | solution.py:655
  50.0 1.2 dynamic-slice_reduce_fusion.tally_ref.refs_2_
  51.3 1.0 copy-done.12
  52.2 11.4 %early.1 = (f32[8200,128]{1,0:T(8,128)S(1)}, f32[8200,128]{1,0:T(8,128)S(1)}, f32[8200,128]{1,0:T(8,128)S(1)}, f32[8200,128]{1,0:T(8,128)S(1)}) custom-call(s32[65536]{0:T(1024)} %bitcast.32, s32[32]{0:T(128)} %fusion.order_ref.refs_1_, s32[32]{0:T(128)} %dynamic-slice_reduce_fusion.tally_ref.refs_2_, s32[32,2,128]{2,1,0:T(2,128)} %slice.13.index_ref.refs_6_, ...), custom_call_target="tpu_custom_call" | custom-call | flops 268435456 | bytes 33554432 | tf_op jit(solution)/shard_map/early/pallas_call | solution.py:374
  63.8 2.6 %collective-permute-done.5.refs_8_ = s32[2048,128]{1,0:T(8,128)S(1)} collective-permute-done((s32[2048,128]{1,0:T(8,128)S(1)}, s32[2048,128]{1,0:T(8,128)S(1)}, u32[]{:S(2)}, u32[]{:S(2)}) %collective-permute-start.5) | collective-permute-done | bytes 1048608 | tf_op jit(solution)/shard_map/ppermute | solution.py:673
  66.4 1.0 copy-done.11
  67.4 21.3 %now.1 = (bf16[16384,256]{1,0:T(8,128)(2,1)}, s32[8,16,1152]{2,1,0:T(8,128)}, f32[8200,128]{1,0:T(8,128)S(1)}, f32[8200,128]{1,0:T(8,128)S(1)}, f32[8200,128]{1,0:T(8,128)S(1)}, /*index=5*/f32[8200,128]{1,0:T(8,128)S(1)}) custom-call(s32[65536]{0:T(1024)} %bitcast.33, ...), custom_call_target="tpu_custom_call", output_to_operand_aliasing={{2}: (11, {}), {3}: (12, {}), {4}: (13, {}), {5}: (14, {})} | custom-call | flops 1073741824 | bytes 83886080 | tf_op jit(solution)/shard_map/now/pallas_call | solution.py:498
  88.7 8.2 %all-to-all-start.1 = ((s32[8,16,1152]{2,1,0:T(8,128)}), s32[8,16,1152]{2,1,0:T(8,128)S(1)}, u32[]{:S(2)}, u32[]{:S(2)}) async-start(s32[8,16,1152]{2,1,0:T(8,128)} %get-tuple-element.81), calls=%async_computation.1 | async-start | bytes 1179648 | tf_op jit(solution)/shard_map/all_to_all | solution.py:679
  96.9 0.8 constant_dynamic-slice_fusion
  97.7 14.4 %all-to-all-done.1.got_ref = s32[8,16,1152]{2,1,0:T(8,128)S(1)} async-done(((s32[8,16,1152]{2,1,0:T(8,128)}), s32[8,16,1152]{2,1,0:T(8,128)S(1)}, u32[]{:S(2)}, u32[]{:S(2)}) %all-to-all-start.1) | async-done | bytes 589856 | tf_op jit(solution)/shard_map/all_to_all | solution.py:679
  112.1 2.1 %sum.1 = f32[32,1024]{1,0:T(8,128)S(1)} custom-call(s32[8,16,1152]{2,1,0:T(8,128)S(1)} %all-to-all-done.1.got_ref), custom_call_target="tpu_custom_call" | custom-call | tf_op jit(solution)/shard_map/sum/pallas_call | solution.py:549
  114.2 6.5 %all-gather = f32[128,1024]{1,0:T(8,128)S(1)} all-gather(f32[32,1024]{1,0:T(8,128)S(1)} %sum.1), channel_id=2, replica_groups=mesh['row'=4,'col'=8] {'row'}, dimensions={0}, use_global_device_ids=true | all-gather | bytes 655360 | tf_op jit(solution)/shard_map/all_gather | solution.py:681
  120.7 5.5 %drops.1 = f32[32,2048]{1,0:T(8,128)S(1)} custom-call(s32[2,2048]{1,0:T(2,128)S(1)} %bitcast.29, f32[4,32,1024]{2,1,0:T(8,128)S(1)} %bitcast.27), custom_call_target="tpu_custom_call" | custom-call | tf_op jit(solution)/shard_map/drops/pallas_call | solution.py:585
  126.3 12.9 %all_to_all.22 = f32[8,32,256]{2,1,0:T(8,128)S(1)} all-to-all(f32[8,32,256]{2,1,0:T(8,128)S(1)} %bitcast.34), channel_id=1, replica_groups=mesh['row'=4,'col'=8] {'col'}, dimensions={0} | all-to-all | bytes 524288 | tf_op jit(solution)/shard_map/all_to_all | solution.py:685
  139.1 0.8 copy.19
  (44 shorter events, 2.1 us)
Async XLA Ops:
  0.6 1.0 copy-start.1
  1.7 9.2 %collective-permute-start = (s32[256,128]{1,0:T(8,128)S(1)}, s32[256,128]{1,0:T(8,128)S(1)}, u32[]{:S(2)}, u32[]{:S(2)}) collective-permute-start(s32[256,128]{1,0:T(8,128)S(1)} %get-tuple-element.43), channel_id=1, source_target_pairs={{0,2},{1,3},{2,0},{3,1},{4,6},{5,7},{6,4},{7,5},{8,24},{9,25},{10,... | collective-permute-start | bytes 393224 | tf_op jit(solution)/shard_map/ppermute | solution.py:638
  8.8 0.7 copy-start.4
  9.5 0.7 copy-start.5
  10.9 16.1 %collective-permute-start.1 = (s32[512,128]{1,0:T(8,128)S(1)}, s32[512,128]{1,0:T(8,128)S(1)}, u32[]{:S(2)}, u32[]{:S(2)}) collective-permute-start(s32[512,128]{1,0:T(8,128)S(1)} %pad_add_fusion.2), channel_id=1, source_target_pairs={{0,4},{1,5},{2,6},{3,7},{4,0},{5,1},{6,2},{7,3},{8,10},{9,11},{10,... | collective-permute-start | bytes 786440 | tf_op jit(solution)/shard_map/ppermute | solution.py:638
  13.7 0.7 copy-start.2
  14.4 0.7 copy-start.6
  15.1 18.6 %copy-start.3 = (s32[272]{0:T(512)S(1)}, s32[272]{0:T(512)}, u32[]{:S(2)}) copy-start(s32[272]{0:T(512)} %get-tuple-element.52.todo_ref) | copy-start | bytes 3268
  15.1 18.6 %copy-start.7 = (s32[69]{0:T(128)S(1)}, s32[69]{0:T(128)}, u32[]{:S(2)}) copy-start(s32[69]{0:T(128)} %get-tuple-element.53.owner_ref) | copy-start | bytes 832
  27.1 19.9 %collective-permute-start.2 = (s32[1024,128]{1,0:T(8,128)S(1)}, s32[1024,128]{1,0:T(8,128)S(1)}, u32[]{:S(2)}, u32[]{:S(2)}) collective-permute-start(s32[1024,128]{1,0:T(8,128)S(1)} %pad_add_fusion.1), channel_id=1, source_target_pairs={{0,1},{1,0},{2,3},{3,2},{4,5},{5,4},{6,7},{7,6},{8,12},{9,13},{10,... | collective-permute-start | bytes 1572872 | tf_op jit(solution)/shard_map/ppermute | solution.py:638
  29.8 17.2 %all-to-all-start = ((s32[32,16,128]{2,1,0:T(8,128)}), s32[32,16,128]{2,1,0:T(8,128)S(1)}, u32[]{:S(2)}, u32[]{:S(2)}) async-start(s32[32,16,128]{2,1,0:T(8,128)} %bitcast.3), calls=%async_computation | async-start | bytes 524288 | tf_op jit(solution)/shard_map/all_to_all | solution.py:608
  46.0 1.0 copy-start
  47.0 4.2 %copy-start.9 = (s32[32,16,128]{2,1,0:T(8,128)}, s32[32,16,128]{2,1,0:T(8,128)S(1)}, u32[]{:S(2)}) copy-start(s32[32,16,128]{2,1,0:T(8,128)S(1)} %all-to-all-done) | copy-start | bytes 786436
  47.1 4.2 %copy-start.8 = (s32[2048,128]{1,0:T(8,128)}, s32[2048,128]{1,0:T(8,128)S(1)}, u32[]{:S(2)}) copy-start(s32[2048,128]{1,0:T(8,128)S(1)} %pad_add_fusion.one_ref) | copy-start | bytes 3145732
  47.1 4.1 %collective-permute-start.4 = (s32[2048,128]{1,0:T(8,128)S(1)}, s32[2048,128]{1,0:T(8,128)S(1)}, u32[]{:S(2)}, u32[]{:S(2)}) collective-permute-start(s32[2048,128]{1,0:T(8,128)S(1)} %pad_add_fusion.one_ref), channel_id=1, source_target_pairs={{0,8},{1,9},{2,10},{3,11},{4,12},{5,13},{6,14},{7,15},{8,0},{9,1},... | collective-permute-start | bytes 3145736 | tf_op jit(solution)/shard_map/ppermute | solution.py:656
  47.8 15.8 %collective-permute-start.3 = (s32[2048,128]{1,0:T(8,128)S(1)}, s32[2048,128]{1,0:T(8,128)S(1)}, u32[]{:S(2)}, u32[]{:S(2)}) collective-permute-start(s32[2048,128]{1,0:T(8,128)S(1)} %pad_add_fusion.one_ref), channel_id=1, source_target_pairs={{0,16},{1,17},{2,18},{3,19},{4,20},{5,21},{6,22},{7,23},{8,9},{9,8... | collective-permute-start | bytes 3145736 | tf_op jit(solution)/shard_map/ppermute | solution.py:655
  51.3 1.0 copy-start.12
  63.7 2.7 %copy-start.10 = (s32[2048,128]{1,0:T(8,128)}, s32[2048,128]{1,0:T(8,128)S(1)}, u32[]{:S(2)}) copy-start(s32[2048,128]{1,0:T(8,128)S(1)} %collective-permute-done.3.refs_7_) | copy-start | bytes 3145732
  63.7 2.7 %collective-permute-start.5 = (s32[2048,128]{1,0:T(8,128)S(1)}, s32[2048,128]{1,0:T(8,128)S(1)}, u32[]{:S(2)}, u32[]{:S(2)}) collective-permute-start(s32[2048,128]{1,0:T(8,128)S(1)} %collective-permute-done.3.refs_7_), channel_id=1, source_target_pairs={{0,8},{1,9},{2,10},{3,11},{4,12},{5,13},{6,14},{7,15},{8,0},{9,1},... | collective-permute-start | bytes 3145736 | tf_op jit(solution)/shard_map/ppermute | solution.py:673
  66.4 1.0 copy-start.11
  88.7 23.4 %all-to-all-start.1 = ((s32[8,16,1152]{2,1,0:T(8,128)}), s32[8,16,1152]{2,1,0:T(8,128)S(1)}, u32[]{:S(2)}, u32[]{:S(2)}) async-start(s32[8,16,1152]{2,1,0:T(8,128)} %get-tuple-element.81), calls=%async_computation.1 | async-start | bytes 1179648 | tf_op jit(solution)/shard_map/all_to_all | solution.py:679

commit v3 on v2

--- a/solution.py
+++ b/solution.py
@@ -53,6 +53,33 @@
 
 def pair(low, high):
     return lax.bitwise_or(lax.shift_left(high, 16), lax.bitwise_and(low, 0xFFFF))
+
+
+def coded_rows(values):
+    mean = jnp.sum(values, axis=1, keepdims=True) * (1.0 / values.shape[1])
+    rest = values - mean
+    index, inverse = scale_of(rest)
+    mean_index, mean_inverse = scale_of(mean)
+    mean_code = jnp.floor(mean * mean_inverse * MEAN).astype(I32)
+    lane = lax.broadcasted_iota(I32, (values.shape[0], LANES), 1)
+    head = jnp.where(lane == 0, index, jnp.where(lane == 1, mean_index, mean_code))
+    return coded(rest, inverse), head
+
+
+def both_heads(low, high):
+    return jnp.concatenate([low[:, : LANES // 2], high[:, : LANES // 2]], axis=1)
+
+
+def scale_and_mean(head, side):
+    up, _ = powers()
+    lane = lax.broadcasted_iota(I32, (head.shape[0], LANES), 1)
+
+    def power(index):
+        return jnp.sum(jnp.where(lane == index, up, 0.0), axis=1, keepdims=True)
+
+    at = side * (LANES // 2)
+    mean = head[:, at + 2 : at + 3].astype(F32) * (power(head[:, at + 1 : at + 2]) * (1.0 / MEAN))
+    return power(head[:, at : at + 1]) * (1.0 / FULL), mean
 
 
 def low_of(words):
@@ -162,15 +189,19 @@
     return found
 
 
-def sources(row_count, col_count):
-    orders, core = routes(row_count, col_count)
-    devices = row_count * col_count
-    table = np.zeros((devices, 2, 2, devices // 4), np.int32)
-    for me in range(devices):
-        for far, holder in enumerate((me, me ^ core)):
-            found = [holder ^ mask for mask in masks(orders[1 if holder & core else 0])]
-            table[me, :, far] = np.reshape(found, (2, devices // 4))
-    return table.reshape(devices, devices)
+def mask_table(row_count, col_count):
+    orders, _ = routes(row_count, col_count)
+    return jnp.asarray(np.array([masks(order) for order in orders], np.int32))
+
+
+def source_at(mask_ref, first, place):
+    half = mask_ref.shape[1]
+    col_count = lax.axis_size("col")
+    me = lax.axis_index("row") * col_count + lax.axis_index("col")
+    far = place // (half // 2)
+    holder = lax.bitwise_xor(me, far * col_count)
+    family = lax.bitwise_and(lax.shift_right_logical(holder, log2(col_count)), 1)
+    return lax.bitwise_xor(holder, mask_ref[family, first + lax.rem(place, half // 2)])
 
 
 def gather_steps(row_count, col_count):
@@ -183,15 +214,16 @@
     return pairs, sibling
 
 
-def past_kernel(block, slots, part, parts, todo_ref, owner_ref, start_ref, history_ref, coef_ref, out_ref, coef, source_of, sems):
+def past_kernel(block, slots, region, part, parts, todo_ref, owner_ref, start_ref, history_ref, coef_ref, out_ref, coef, source_of, sems):
     count = owner_ref[owner_ref.shape[0] - 1]
     first, last = count * part // parts, count * (part + 1) // parts
 
     def copies(t):
         slot = lax.rem(t, slots)
-        i = owner_ref[t]
+        group = owner_ref[t]
+        i = lax.shift_right_logical(group, log2(region))
         for g in range(GROUP):
-            entry = jnp.maximum(todo_ref[t * GROUP + g], 0)
+            entry = jnp.maximum(todo_ref[group + g], 0)
             k = lax.shift_right_logical(entry, 3)
             rows = pl.ds(pl.multiple_of(k * block, block), block)
             yield pltpu.make_async_copy(
@@ -222,12 +254,13 @@
         for copy in copies(t):
             copy.wait()
         slot = lax.rem(t, slots)
+        group = owner_ref[t]
         for g in range(1, GROUP):
-            @pl.when(todo_ref[t * GROUP + g] < 0)
+            @pl.when(todo_ref[group + g] < 0)
             def _():
                 source_of[slot, g * block : (g + 1) * block, :] = jnp.zeros((block, source_of.shape[2]), BF16)
 
-        out_ref[owner_ref[t]] += jnp.dot(coef[slot], source_of[slot], preferred_element_type=F32)
+        out_ref[lax.shift_right_logical(group, log2(region))] += jnp.dot(coef[slot], source_of[slot], preferred_element_type=F32)
 
 
 def past_product(todo, owner, coefficients, history, start, block, part, parts):
@@ -237,7 +270,7 @@
     smem = pl.BlockSpec(memory_space=pltpu.SMEM)
     hbm = pl.BlockSpec(memory_space=pl.ANY)
     return pl.pallas_call(
-        functools.partial(past_kernel, block, slots, part, parts),
+        functools.partial(past_kernel, block, slots, region_of(coefficients.shape[1] // block), part, parts),
         out_shape=jax.ShapeDtypeStruct(start.shape, F32),
         in_specs=[smem, smem, *vmem(1), hbm, hbm],
         out_specs=vmem()[0],
@@ -251,47 +284,55 @@
             flops=2 * coefficients.size * scenarios // parts, bytes_accessed=moved, transcendentals=0
         ),
         name="past",
-    )(todo, owner, start, history, coefficients)
-
-
-def scan_kernel(delays_ref, now_ref, now_owner_ref, past_ref, past_owner_ref):
+    )(*(pltpu.with_memory_space_constraint(x, pltpu.HBM) for x in (todo, owner)), start, history, coefficients)
+
+
+def scan_kernel(region, delays_ref, now_ref, now_group_ref, past_ref, past_group_ref):
     row_blocks, col_blocks = delays_ref.shape
-    found = (jnp.int32(0), jnp.int32(0))
-    lists, owners = (now_ref, past_ref), (now_owner_ref, past_owner_ref)
-    for i in range(row_blocks):
-        first = [at // GROUP for at in found]
-
-        def look(k, at, i=i):
-            now, past = at
+
+    def look(k, found):
+        found = list(found)
+        delays = [[delays_ref[i, k * GROUP + g] for i in range(row_blocks)] for g in range(GROUP)]
+        for g in range(GROUP):
+            for i in range(row_blocks):
+                delay = delays[g][i]
+                here = jnp.where(delay == 0, 1, 0)
+                now_ref[found[2 * i]] = k * GROUP + g
+                past_ref[found[2 * i + 1]] = (k * GROUP + g) * 8 + delay - 1
+                found[2 * i] += here
+                found[2 * i + 1] += 1 - here
+        return tuple(found)
+
+    starts = tuple(jnp.int32(region * (n // 2)) for n in range(2 * row_blocks))
+    found = lax.fori_loop(0, col_blocks // GROUP, look, starts)
+    for n, (blocks, groups) in enumerate(((now_ref, now_group_ref), (past_ref, past_group_ref))):
+        total = jnp.int32(0)
+        for i in range(row_blocks):
+            end = found[2 * i + n]
             for g in range(GROUP):
-                delay = delays_ref[i, k * GROUP + g]
-                here = jnp.where(delay == 0, 1, 0)
-                now_ref[now] = k * GROUP + g
-                past_ref[past] = (k * GROUP + g) * 8 + delay - 1
-                now, past = now + here, past + (1 - here)
-            return now, past
-
-        found = lax.fori_loop(0, col_blocks // GROUP, look, found)
-        for g in range(GROUP):
-            now_ref[found[0] + g] = -1
-            past_ref[found[1] + g] = -1
-        found = tuple((at + (GROUP - 1)) // GROUP * GROUP for at in found)
-        for n in range(2):
-            @pl.loop(first[n], found[n] // GROUP)
+                blocks[end + g] = -1
+            number = (end - region * i + (GROUP - 1)) // GROUP
+
+            @pl.loop(0, number)
             def _(t):
-                owners[n][t] = i
-
-    for n in range(2):
-        owners[n][owners[n].shape[0] - 1] = found[n] // GROUP
+                groups[total + t] = region * i + t * GROUP
+
+            total = total + number
+        groups[groups.shape[0] - 1] = total
+
+
+def region_of(col_blocks):
+    return 1 << (col_blocks + GROUP - 1).bit_length()
 
 
 def scan(delays):
     row_blocks, col_blocks = delays.shape
+    region = region_of(col_blocks)
     groups = row_blocks * (col_blocks // GROUP + 1)
     smem = pl.BlockSpec(memory_space=pltpu.SMEM)
-    one = (jax.ShapeDtypeStruct((groups * GROUP,), I32), jax.ShapeDtypeStruct((groups + 1,), I32))
+    one = (jax.ShapeDtypeStruct((row_blocks * region,), I32), jax.ShapeDtypeStruct((groups + 1,), I32))
     return pl.pallas_call(
-        scan_kernel,
+        functools.partial(scan_kernel, region),
         out_shape=one + one,
         in_specs=[smem],
         out_specs=(smem,) * 4,
@@ -306,10 +347,14 @@
     ]
 
 
-def decode(index_ref, order_ref, first, blocks, branch_rows, skip, codes, rows):
+def decode(head, mask_ref, first, blocks, sizes, skip, codes, rows):
+    branch_rows = sizes[2]
+
     @pl.loop(0, blocks)
     def _(place):
-        scales, _ = powers(exponent=index_ref[order_ref[first + place]])
+        source = source_at(mask_ref, first, skip + place)
+        at = (sizes[0] * CHAINS // LANES) % 8 + 1
+        scales, _ = powers(exponent=head[source, at : at + 2, :])
         scales = scales * (1.0 / FULL)
         words = codes[pl.ds(pl.multiple_of((skip + place) * branch_rows, branch_rows), branch_rows), :]
         base = place * (4 * branch_rows)
@@ -319,17 +364,21 @@
             rows[pl.ds(base + 2 * branch_rows + side, branch_rows, stride=2), :] = -value
 
 
-def scatter(sizes, first, blocks, lists_ref, order_ref, tally_ref, rows, acc):
+def scatter(sizes, first, skip, blocks, lists_ref, mask_ref, rows, acc):
     capacity, words, branch_rows = sizes
     bits = node_bits(acc[0].shape[0] // 2 - PAD)
 
     @pl.loop(0, blocks)
     def _(place):
-        source = order_ref[first + place]
+        source = source_at(mask_ref, first, skip + place)
         base = place * (4 * branch_rows)
         start = source * words
-
-        @pl.loop(0, (tally_ref[source] + (UNROLL - 1)) // UNROLL)
+        tally = start + CHAINS * capacity + lax.axis_index("col") * CHAINS
+        most = lists_ref[tally]
+        for chain in range(1, CHAINS):
+            most = jnp.maximum(most, lists_ref[tally + chain])
+
+        @pl.loop(0, (most + (UNROLL - 1)) // UNROLL)
         def _(j):
             for u in range(UNROLL):
                 after = []
@@ -342,18 +391,29 @@
                     part[at, :] = value
 
 
-def add_ends(sizes, first, lists_ref, order_ref, tally_ref, index_ref, codes, rows, acc):
+def head_copy(sizes, message_ref, head, sem):
+    first = sizes[0] * CHAINS // LANES // 8 * 8
+    return pltpu.make_async_copy(message_ref.at[:, pl.ds(first, head.shape[1])], head, sem)
+
+
+def head_shape(sizes, devices):
+    first = sizes[0] * CHAINS // LANES // 8 * 8
+    return pltpu.VMEM((devices, sizes[1] // LANES - first, LANES), I32)
+
+
+def add_ends(sizes, late, lists_ref, mask_ref, head, codes, rows, acc):
     branch_rows = sizes[2]
+    first = late * (mask_ref.shape[1] // 2)
     blocks = codes.shape[0] // branch_rows
     batch = rows.shape[0] // (4 * branch_rows)
     for skip in range(0, blocks, batch):
-        decode(index_ref, order_ref, first + skip, batch, branch_rows, skip, codes, rows)
-        scatter(sizes, first + skip, batch, lists_ref, order_ref, tally_ref, rows, acc)
-
-
-def early_kernel(sizes, lists_ref, order_ref, tally_ref, index_ref, one_ref, two_ref, *more):
-    acc, (codes, rows, sems) = more[:CHAINS], more[CHAINS:]
-    copies = row_copies((one_ref, two_ref), codes, sems)
+        decode(head, mask_ref, first, batch, sizes, skip, codes, rows)
+        scatter(sizes, first, skip, batch, lists_ref, mask_ref, rows, acc)
+
+
+def early_kernel(sizes, lists_ref, mask_ref, message_ref, one_ref, two_ref, *more):
+    acc, (codes, rows, head, sems) = more[:CHAINS], more[CHAINS:]
+    copies = [*row_copies((one_ref, two_ref), codes, sems), head_copy(sizes, message_ref, head, sems.at[2])]
     for copy in copies:
         copy.start()
     clear = 512
@@ -365,47 +425,54 @@
             part[pl.ds(pl.multiple_of(n * clear + 2 * PAD, 8), clear), :] = jnp.zeros((clear, LANES), F32)
     for copy in copies:
         copy.wait()
-    add_ends(sizes, 0, lists_ref, order_ref, tally_ref, index_ref, codes, rows, acc)
-
-
-def early_scatter(lists, order, tally, index, pieces, nodes, sizes):
+    add_ends(sizes, 0, lists_ref, mask_ref, head, codes, rows, acc)
+
+
+def scatter_room(pieces, sizes, devices):
+    rows = min(2 * pieces[0].shape[0], 16 * sizes[2])
+    return [
+        pltpu.VMEM((2 * pieces[0].shape[0], LANES), I32),
+        pltpu.VMEM((4 * rows, LANES), F32),
+        head_shape(sizes, devices),
+    ], (2 * pieces[0].shape[0] + 4 * rows + devices * 16) * LANES * 4 >> 20
+
+
+def early_scatter(message, mask, pieces, nodes, sizes):
+    room, mib = scatter_room(pieces, sizes, message.shape[0])
     smem = pl.BlockSpec(memory_space=pltpu.SMEM)
     hbm = pl.BlockSpec(memory_space=pl.ANY)
     return pl.pallas_call(
         functools.partial(early_kernel, sizes),
         out_shape=tuple(pltpu.VMEM((2 * (nodes // CHAINS + PAD), LANES), F32) for _ in range(CHAINS)),
-        in_specs=[smem] * 3 + vmem(1) + [hbm] * 2,
+        in_specs=[smem] * 2 + [hbm] * 3,
         out_specs=tuple(vmem(CHAINS)),
-        scratch_shapes=[
-            pltpu.VMEM((2 * pieces[0].shape[0], pieces[0].shape[1]), I32),
-            pltpu.VMEM((4 * min(2 * pieces[0].shape[0], 16 * sizes[2]), LANES), F32),
-            pltpu.SemaphoreType.DMA((2,)),
-        ],
-        compiler_params=params(38),
+        scratch_shapes=[*room, pltpu.SemaphoreType.DMA((3,))],
+        compiler_params=params(mib + 4),
         cost_estimate=pl.CostEstimate(flops=1 << 28, bytes_accessed=32 << 20, transcendentals=0),
         name="early",
-    )(lists, order, tally, index, *pieces)
+    )(message.reshape(-1), mask, message, *pieces)
 
 
 def now_kernel(
     block, slots, chunks, sizes,
-    lists_ref, order_ref, tally_ref, todo_ref, owner_ref, past_ref, index_ref,
+    lists_ref, mask_ref, todo_ref, owner_ref, past_ref, message_ref,
     one_ref, two_ref, history_ref, coef_ref,
     charge_ref, out_ref, acc,
-    codes, rows, charge, coef, source_of, total, row_sem, load_sem, store_sem, coef_sem,
+    codes, rows, head, charge, coef, source_of, total, row_sem, load_sem, store_sem, coef_sem,
 ):
     row_blocks, col_blocks = total.shape[0], charge.shape[0] // block
-    copies = row_copies((one_ref, two_ref), codes, row_sem)
+    copies = [*row_copies((one_ref, two_ref), codes, row_sem), head_copy(sizes, message_ref, head, row_sem.at[2])]
     for copy in copies:
         copy.start()
     load = pltpu.make_async_copy(history_ref.at[0], charge, load_sem)
     load.start()
 
     count = owner_ref[owner_ref.shape[0] - 1]
+    region_bits = log2(region_of(col_blocks))
 
     def coef_copy(t, g):
-        i = owner_ref[t]
-        k = jnp.maximum(todo_ref[t * GROUP + g], 0)
+        i = lax.shift_right_logical(owner_ref[t], region_bits)
+        k = jnp.maximum(todo_ref[owner_ref[t] + g], 0)
         slot = lax.rem(t, slots)
         return pltpu.make_async_copy(
             coef_ref.at[pl.ds(pl.multiple_of(i * block, block), block),
@@ -421,7 +488,7 @@
 
     for copy in copies:
         copy.wait()
-    add_ends(sizes, order_ref.shape[0] // 2, lists_ref, order_ref, tally_ref, index_ref, codes, rows, acc)
+    add_ends(sizes, 1, lists_ref, mask_ref, head, codes, rows, acc)
     load.wait()
 
     def store(k):
@@ -445,13 +512,13 @@
     @pl.loop(0, count)
     def _(t):
         for g in range(GROUP):
-            k = todo_ref[t * GROUP + g]
+            k = todo_ref[owner_ref[t] + g]
             held = charge[pl.ds(pl.multiple_of(jnp.maximum(k, 0) * block, block), block), :]
             source_of[g * block : (g + 1) * block, :] = jnp.where(k >= 0, held, jnp.zeros_like(held))
         for g in range(GROUP):
             coef_copy(t, g).wait()
         slot = lax.rem(t, slots)
-        total[owner_ref[t]] += jnp.dot(coef[slot], source_of[...], preferred_element_type=F32)
+        total[lax.shift_right_logical(owner_ref[t], region_bits)] += jnp.dot(coef[slot], source_of[...], preferred_element_type=F32)
 
         @pl.when(t + slots < count)
         def _():
@@ -460,27 +527,19 @@
 
     turned = jnp.concatenate([total[i].T for i in range(row_blocks)], axis=1)
     nodes = turned.shape[1]
-    mean = jnp.sum(turned, axis=1, keepdims=True) * (1.0 / nodes)
-    rest = turned - mean
-    index, inverse = scale_of(rest)
-    codes = coded(rest, inverse)
-    mean_index, mean_inverse = scale_of(mean)
-    mean_code = jnp.floor(mean * mean_inverse * MEAN).astype(I32)
-    lane = lax.broadcasted_iota(I32, (turned.shape[0], LANES), 1)
-    head = jnp.where(lane == 1, mean_index, mean_code)
-    head = jnp.where(lane == 0, index, head)
+    codes, head = coded_rows(turned)
     chunk = turned.shape[0] // chunks
     half = chunk // 2
     for c in range(chunks):
         one = slice(c * chunk, c * chunk + half)
         two = slice(c * chunk + half, (c + 1) * chunk)
         out_ref[c, :, :nodes] = pair(codes[one], codes[two])
-        out_ref[c, :, nodes:] = jnp.concatenate([head[one, : LANES // 2], head[two, : LANES // 2]], axis=1)
+        out_ref[c, :, nodes:] = both_heads(head[one], head[two])
 
     pltpu.make_async_copy(charge, charge_ref, store_sem).wait()
 
 
-def now_product(lists, order, tally, index, todo, owner, past, acc, pieces, history, coefficients, block, chunks, sizes):
+def now_product(message, mask, todo, owner, past, acc, pieces, history, coefficients, block, chunks, sizes):
     row_blocks, _, scenarios = past.shape
     rows = row_blocks * block
     nodes = history.shape[1]
@@ -488,7 +547,9 @@
     smem = pl.BlockSpec(memory_space=pltpu.SMEM)
     hbm = pl.BlockSpec(memory_space=pl.ANY)
     held = [pltpu.with_memory_space_constraint(part, pltpu.VMEM) for part in acc]
-    before, count = 11, len(acc)
+    before, count = 10, len(acc)
+    room, mib = scatter_room(pieces, sizes, message.shape[0])
+    mib += (nodes * 2 + rows * 4 * 6) * scenarios + slots * GROUP * block * block * 2 >> 20
 
     def kernel(*refs):
         sums = refs[before + count + 2 : before + 2 * count + 2]
@@ -502,53 +563,47 @@
             jax.ShapeDtypeStruct((chunks, scenarios // chunks // 2, rows + LANES), I32),
             *[pltpu.VMEM(part.shape, F32) for part in acc],
         ),
-        in_specs=[smem] * 5 + vmem(2) + [hbm] * 4 + vmem(count),
+        in_specs=[smem] * 4 + vmem(1) + [hbm] * 5 + vmem(count),
         out_specs=(hbm, *vmem(1 + count)),
         input_output_aliases={before + n: 2 + n for n in range(count)},
         scratch_shapes=[
-            pltpu.VMEM((2 * pieces[0].shape[0], scenarios // 2), I32),
-            pltpu.VMEM((4 * min(2 * pieces[0].shape[0], 16 * sizes[2]), LANES), F32),
+            *room,
             pltpu.VMEM((nodes, scenarios), BF16),
             pltpu.VMEM((slots, block, GROUP * block), BF16),
             pltpu.VMEM((GROUP * block, scenarios), BF16),
             pltpu.VMEM((row_blocks, block, scenarios), F32),
-            pltpu.SemaphoreType.DMA((2,)),
+            pltpu.SemaphoreType.DMA((3,)),
             pltpu.SemaphoreType.DMA,
             pltpu.SemaphoreType.DMA,
             pltpu.SemaphoreType.DMA((slots, GROUP)),
         ],
-        compiler_params=params(40),
+        compiler_params=params(mib + 6),
         cost_estimate=pl.CostEstimate(flops=1 << 30, bytes_accessed=80 << 20, transcendentals=0),
         name="now",
-    )(lists, order, tally, todo, owner, past, index, *pieces, history, coefficients, *held)[:2]
+    )(message.reshape(-1), mask, todo, owner, past, message, *pieces, history, coefficients, *held)[:2]
 
 
 def sum_kernel(got_ref, out_ref):
     sources, half, width = got_ref.shape
     nodes = width - LANES
-    up, _ = powers()
-    lane = lax.broadcasted_iota(I32, (half, LANES), 1)
-
-    def power(index):
-        return jnp.sum(jnp.where(lane == index, up, 0.0), axis=1, keepdims=True)
-
+    codes, heads = [], []
     for side in range(2):
         total = jnp.zeros((half, nodes), F32)
         for source in range(sources):
             words = got_ref[source, :, :nodes]
-            head = got_ref[source, :, nodes:]
-            at = side * (LANES // 2)
-            codes = (high_of(words) if side else low_of(words)).astype(F32)
-            mean = head[:, at + 2 : at + 3].astype(F32) * (power(head[:, at + 1 : at + 2]) * (1.0 / MEAN))
-            total = total + (codes * (power(head[:, at : at + 1]) * (1.0 / FULL)) + mean)
-        out_ref[side * half : (side + 1) * half, :] = total
+            scale, mean = scale_and_mean(got_ref[source, :, nodes:], side)
+            total = total + ((high_of(words) if side else low_of(words)).astype(F32) * scale + mean)
+        code, head = coded_rows(total)
+        codes.append(code)
+        heads.append(head)
+    out_ref[:, :nodes] = pair(*codes)
+    out_ref[:, nodes:] = both_heads(*heads)
 
 
 def sum_columns(got):
-    _, half, width = got.shape
     return pl.pallas_call(
         sum_kernel,
-        out_shape=jax.ShapeDtypeStruct((2 * half, width - LANES), F32),
+        out_shape=jax.ShapeDtypeStruct(got.shape[1:], I32),
         in_specs=vmem(1),
         out_specs=vmem()[0],
         compiler_params=params(16),
@@ -556,40 +611,50 @@
     )(got)
 
 
-def drop_kernel(node_ref, potential_ref, out_ref):
-    row_count, excitations, nodes = potential_ref.shape
+def drop_kernel(node_ref, word_ref, out_ref):
+    row_count, half, width = word_ref.shape
+    nodes = width - LANES
     per_row = nodes // LANES
-    groups = excitations // 8
+    worth = [[scale_and_mean(word_ref[r, :, nodes:], side) for side in range(2)] for r in range(row_count)]
 
     @pl.loop(0, node_ref.shape[1] // LANES)
     def _(group):
         at = pl.ds(pl.multiple_of(group * LANES, LANES), LANES)
-        found = [[None] * groups, [None] * groups]
+        found = []
         for end in range(2):
             node = jnp.broadcast_to(node_ref[pl.ds(end, 1), at], (8, LANES))
             inner = lax.bitwise_and(node, LANES - 1)
             outer = lax.shift_right_logical(node, log2(LANES))
-            for e in range(groups):
-                value = jnp.zeros((8, LANES), F32)
-                for h in range(row_count * per_row):
-                    lanes = slice(h % per_row * LANES, (h % per_row + 1) * LANES)
-                    held = potential_ref[h // per_row, e * 8 : (e + 1) * 8, lanes]
-                    seen = jnp.take_along_axis(held, inner, axis=1, mode="promise_in_bounds")
-                    value = jnp.where(outer == h, seen, value)
-                found[end][e] = value
+            row = lax.shift_right_logical(node, log2(nodes))
+            for e in range(0, half, 8):
+                values = [jnp.zeros((8, LANES), F32)] * 2
+                for r in range(row_count):
+                    word = jnp.zeros((8, LANES), I32)
+                    for h in range(per_row):
+                        held = word_ref[r, e : e + 8, h * LANES : (h + 1) * LANES]
+                        seen = jnp.take_along_axis(held, inner, axis=1, mode="promise_in_bounds")
+                        word = jnp.where(outer == r * per_row + h, seen, word)
+                    for side, code in enumerate((low_of(word), high_of(word))):
+                        scale, mean = worth[r][side]
+                        value = code.astype(F32) * scale[e : e + 8] + mean[e : e + 8]
+                        values[side] = jnp.where(row == r, value, values[side])
+                found.append(values)
+        groups = len(found) // 2
         for e in range(groups):
-            out_ref[e * 8 : (e + 1) * 8, at] = found[0][e] - found[1][e]
-
-
-def row_drops(nodes, potentials):
+            for side in range(2):
+                rows = pl.ds(side * half + e * 8, 8)
+                out_ref[rows, at] = found[e][side] - found[groups + e][side]
+
+
+def row_drops(nodes, words):
     return pl.pallas_call(
         drop_kernel,
-        out_shape=jax.ShapeDtypeStruct((potentials.shape[1], nodes.shape[1]), F32),
+        out_shape=jax.ShapeDtypeStruct((2 * words.shape[1], nodes.shape[1]), F32),
         in_specs=vmem(2),
         out_specs=vmem()[0],
         compiler_params=params(24),
         name="drops",
-    )(nodes, potentials)
+    )(nodes, words)
 
 
 def branch_lists(index, owner, slot, slab_owner, slab_offset, col_count, share, sizes):
@@ -630,7 +695,6 @@
         return past_product(late, late_owner, coefficients, history, past, block, part, parts)
 
     held, index = pack(currents)
-    order = lax.dynamic_slice_in_dim(jnp.asarray(sources(row_count, col_count)), me, 1, 0)[0]
     jobs = {1: (0,), 2: (1,)}
     message = None
     for number, step in enumerate(pairs[:-1]):
@@ -647,7 +711,7 @@
             got, past, lists, tally, slab, late = together((got, past, lists, tally, slab, late))
             message = share_lists(lists, tally, slab, row_count, col_count)
         elif number == len(pairs) - 2:
-            got, past, message, order = together((got, past, message, order))
+            got, past, message = together((got, past, message))
         else:
             got, past = together((got, past))
         held = jnp.concatenate([held, got], axis=0)
@@ -660,19 +724,17 @@
     slab_tiles = 2 * slab_rows // LANES
     width = message.shape[0] // devices
     message = message.reshape(devices, width, LANES)
-    tally = lax.dynamic_slice_in_dim(message[:, list_tiles], my_col * CHAINS, CHAINS, 1).max(axis=1)
     row_slab = lax.dynamic_slice_in_dim(message, my_row * col_count, col_count, 0)
     row_slab = row_slab[:, list_tiles + 3 : list_tiles + 3 + slab_tiles]
-    index = message[:, list_tiles + 1 : list_tiles + 3]
     row_slab = row_slab.reshape(col_count, 2, slab_rows).transpose(1, 0, 2).reshape(2, col_count * slab_rows)
 
-    lists = message.reshape(-1)
+    mask = mask_table(row_count, col_count)
     sizes = (capacity, width * LANES, branch_rows)
-    acc = early_scatter(lists, order, tally, index, (held, far), history.shape[1], sizes)
+    acc = early_scatter(message, mask, (held, far), history.shape[1], sizes)
     mid, past, acc = together((mid, past, acc))
     last = lax.ppermute(mid, ALL, sibling)
     charge, partial = now_product(
-        lists, order, tally, index, todo, owner, past, acc, (mid, last), history, coefficients,
+        message, mask, todo, owner, past, acc, (mid, last), history, coefficients,
         block, col_count, sizes,
     )
 

time: 141 us -> 135 us (0.957)
  waiting for transfers between devices: 17 us -> 25.2 us
  local copies, waits for them, and re-layouts: 11 us -> 4.11 us
  Pallas kernels: 68.7 us -> 65.3 us
  starting transfers between devices: 20.9 us -> 18.8 us
    unnamed x28 -> x14, local copies, waits for them, and re-layouts: 7.47 us -> 3.16 us
    ppermute x1, waiting for transfers between devices: 0.01 us -> 2.54 us  [local(): mid = lax.ppermute(held, ALL, pairs[-1])]
    all_to_all x1, waiting for transfers between devices: 14.4 us -> 16.9 us  [local(): lax.all_to_all(partial, 'col', split_axis=0, concat_axis=0, tiled=True)]
    pallas_call x1, Pallas kernels: 21.3 us -> 19.3 us  [now_product(): pl.pallas_call(kernel, out_shape=(jax.ShapeDtypeStruct((nodes, scenarios)...]
    pallas_call x1, Pallas kernels: 11.4 us -> 9.67 us  [early_scatter(): pl.pallas_call(functools.partial(early_kernel, sizes), out_shape=tuple((p...]
    all_to_all x1, waiting for transfers between devices: 0.01 us -> 1.65 us  [share_lists(): return lax.all_to_all(message, ALL, split_axis=0, concat_axis=0, tiled=True)]
    ppermute x1, waiting for transfers between devices: 0.01 us -> 1.49 us  [local(): far = lax.ppermute(held, ALL, sibling)]
  transfers between devices with their start and end apart: 8 -> 8, of which waited for: 2 -> 5; matrix products, arithmetic and copies ran while one was open for 4% -> 1% of each run, Pallas kernels for 28% -> 29%
where the time goes in v3:
time: 135 us; the launch traced here: 134 us
  Pallas kernels  65.3 us (48%)
  waiting for transfers between devices  25.2 us (19%)
  starting transfers between devices  18.8 us (14%)
  blocking collectives  18.7 us (14%)
  local copies, waits for them, and re-layouts  4.11 us (3%)
    pallas_call x2, Pallas kernels, past_product(): pl.pallas_call(functools.partial(past_kernel, block, slots, region_of(coe...  25 us
    pallas_call x1, Pallas kernels, now_product(): pl.pallas_call(kernel, out_shape=(jax.ShapeDtypeStruct((nodes, scenarios)...  19.3 us
    all_to_all x1, waiting for transfers between devices, local(): lax.all_to_all(partial, 'col', split_axis=0, concat_axis=0, tiled=True)  16.9 us
    all_to_all x1, blocking collectives, local(): lax.all_to_all(found, 'col', split_axis=0, concat_axis=0, tiled=True)  12.9 us
    pallas_call x1, Pallas kernels, early_scatter(): pl.pallas_call(functools.partial(early_kernel, sizes), out_shape=tuple((p...  9.67 us
    ppermute x3, starting transfers between devices, local(): got = lax.ppermute(held, ALL, step)  7.71 us
    all_to_all x1, starting transfers between devices, local(): lax.all_to_all(partial, 'col', split_axis=0, concat_axis=0, tiled=True)  7.28 us
    all_gather x1, blocking collectives, local(): potentials = lax.all_gather(mine, 'row', axis=0, tiled=False)  5.87 us
  transfers between devices with their start and end apart: 8, of which 5 were waited for; matrix products, arithmetic and copies ran while one was open for 1% of the time, Pallas kernels for 29%

profile of v3, /device:TPU:0, one launch (start us, length us, event | category | flops | bytes accessed | tf_op | source)
XLA Modules:
  0.0 133.9 jit_solution(1181712132986154190)
XLA Ops:
  0.6 0.9 copy-done
  1.6 0.1 pack.1
  1.7 3.1 %collective-permute-start = (s32[256,128]{1,0:T(8,128)S(1)}, s32[256,128]{1,0:T(8,128)S(1)}, u32[]{:S(2)}, u32[]{:S(2)}) collective-permute-start(s32[256,128]{1,0:T(8,128)S(1)} %get-tuple-element.42), channel_id=1, source_target_pairs={{0,2},{1,3},{2,0},{3,1},{4,6},{5,7},{6,4},{7,5},{8,24},{9,25},{10,... | collective-permute-start | bytes 393224 | tf_op jit(solution)/shard_map/ppermute | solution.py:702
  4.8 0.7 add_bitcast_fusion
  5.5 3.1 %scan.1 = (s32[512]{0:T(512)}, s32[69]{0:T(128)}, s32[512]{0:T(512)}, s32[69]{0:T(128)}) custom-call(s32[4,64]{1,0:T(4,128)} %delays_ref.1), custom_call_target="tpu_custom_call" | custom-call | tf_op jit(solution)/shard_map/scan/pallas_call | solution.py:334
  8.7 0.7 copy-done.3
  9.3 0.7 copy-done.4
  10.0 0.6 lists.1
  10.7 0.1 pad.6.clone
  10.8 2.7 %collective-permute-start.1 = (s32[512,128]{1,0:T(8,128)S(1)}, s32[512,128]{1,0:T(8,128)S(1)}, u32[]{:S(2)}, u32[]{:S(2)}) collective-permute-start(s32[512,128]{1,0:T(8,128)S(1)} %pad_add_fusion.2), channel_id=1, source_target_pairs={{0,4},{1,5},{2,6},{3,7},{4,0},{5,1},{6,2},{7,3},{8,10},{9,11},{10,... | collective-permute-start | bytes 786440 | tf_op jit(solution)/shard_map/ppermute | solution.py:702
  13.4 0.1 broadcast_in_dim.8.start_ref
  13.5 12.2 %past.2.start_ref = f32[4,256,256]{2,1,0:T(8,128)S(1)} custom-call(s32[512]{0:T(512)} %get-tuple-element.51.todo_ref, s32[69]{0:T(128)} %get-tuple-element.52.owner_ref, f32[4,256,256]{2,1,0:T(8,128)S(1)} %broadcast_in_dim.8.start_ref, bf16[4,16384,256]{2,1,0:T(8,128)(2,1)} %refs_8_.1, bf16[1024,16384]{1,0:T(8,128)(2,1)} %refs_9_.1), custom_call_target="tpu_custom_call" | custom-call | flops 4294967296 | bytes 33554432 | tf_op jit(solution)/shard_map/past/pallas_call | solution.py:272
  25.7 0.1 add_add_fusion
  25.9 2.0 %collective-permute-start.2 = (s32[1024,128]{1,0:T(8,128)S(1)}, s32[1024,128]{1,0:T(8,128)S(1)}, u32[]{:S(2)}, u32[]{:S(2)}) collective-permute-start(s32[1024,128]{1,0:T(8,128)S(1)} %pad_add_fusion.1), channel_id=1, source_target_pairs={{0,1},{1,0},{2,3},{3,2},{4,5},{5,4},{6,7},{7,6},{8,12},{9,13},{10,... | collective-permute-start | bytes 1572872 | tf_op jit(solution)/shard_map/ppermute | solution.py:702
  27.8 0.7 broadcast_in_dim.21
  28.6 2.6 %all-to-all-start = ((s32[32,16,128]{2,1,0:T(8,128)}), s32[32,16,128]{2,1,0:T(8,128)S(1)}, u32[]{:S(2)}, u32[]{:S(2)}) async-start(s32[32,16,128]{2,1,0:T(8,128)} %bitcast.3), calls=%async_computation | async-start | bytes 524288 | tf_op jit(solution)/shard_map/all_to_all | solution.py:673
  31.2 12.8 %past.3.refs_4_ = f32[4,256,256]{2,1,0:T(8,128)S(1)} custom-call(s32[512]{0:T(512)} %get-tuple-element.51.todo_ref, s32[69]{0:T(128)} %get-tuple-element.52.owner_ref, f32[4,256,256]{2,1,0:T(8,128)S(1)} %past.2.start_ref, bf16[4,16384,256]{2,1,0:T(8,128)(2,1)} %refs_8_.1, bf16[1024,16384]{1,0:T(8,128)(2,1)} %refs_9_.1), custom_call_target="tpu_custom_call" | custom-call | flops 4294967296 | bytes 33554432 | tf_op jit(solution)/shard_map/past/pallas_call | solution.py:272
  44.0 1.6 %all-to-all-done = s32[32,16,128]{2,1,0:T(8,128)S(1)} async-done(((s32[32,16,128]{2,1,0:T(8,128)}), s32[32,16,128]{2,1,0:T(8,128)S(1)}, u32[]{:S(2)}, u32[]{:S(2)}) %all-to-all-start) | async-done | bytes 262176 | tf_op jit(solution)/shard_map/all_to_all | solution.py:673
  45.7 0.1 collective-permute-start.4
  45.8 1.2 collective-permute-start.3
  47.0 1.5 %collective-permute-done.4.two_ref = s32[2048,128]{1,0:T(8,128)S(1)} collective-permute-done((s32[2048,128]{1,0:T(8,128)S(1)}, s32[2048,128]{1,0:T(8,128)S(1)}, u32[]{:S(2)}, u32[]{:S(2)}) %collective-permute-start.4) | collective-permute-done | bytes 1048608 | tf_op jit(solution)/shard_map/ppermute | solution.py:720
  48.5 9.7 %early.1 = (f32[8200,128]{1,0:T(8,128)S(1)}, f32[8200,128]{1,0:T(8,128)S(1)}, f32[8200,128]{1,0:T(8,128)S(1)}, f32[8200,128]{1,0:T(8,128)S(1)}) custom-call(s32[65536]{0:T(1024)S(1)} %bitcast.25, s32[2,16]{1,0:T(2,128)S(1)} %copy-done.1, s32[32,16,128]{2,1,0:T(8,128)S(1)} %all-to-all-done, s32[2048,128]{1,0:T(8,128)S(1)} %pad_add_fusion.one_ref, ...), custom_call_target="tpu_custom_call" | custom-call | flops 268435456 | bytes 33554432 | tf_op jit(solution)/shard_map/early/pallas_call | solution.py:444
  58.2 2.5 %collective-permute-done.3.refs_6_ = s32[2048,128]{1,0:T(8,128)S(1)} collective-permute-done((s32[2048,128]{1,0:T(8,128)S(1)}, s32[2048,128]{1,0:T(8,128)S(1)}, u32[]{:S(2)}, u32[]{:S(2)}) %collective-permute-start.3) | collective-permute-done | bytes 1048608 | tf_op jit(solution)/shard_map/ppermute | solution.py:719
  60.7 2.7 %collective-permute-done.5.refs_7_ = s32[2048,128]{1,0:T(8,128)S(1)} collective-permute-done((s32[2048,128]{1,0:T(8,128)S(1)}, s32[2048,128]{1,0:T(8,128)S(1)}, u32[]{:S(2)}, u32[]{:S(2)}) %collective-permute-start.5) | collective-permute-done | bytes 1048608 | tf_op jit(solution)/shard_map/ppermute | solution.py:735
  63.4 19.3 %now.1 = (bf16[16384,256]{1,0:T(8,128)(2,1)}, s32[8,16,1152]{2,1,0:T(8,128)}, f32[8200,128]{1,0:T(8,128)S(1)}, f32[8200,128]{1,0:T(8,128)S(1)}, f32[8200,128]{1,0:T(8,128)S(1)}, /*index=5*/f32[8200,128]{1,0:T(8,128)S(1)}) custom-call(s32[65536]{0:T(1024)S(1)} %bitcast.26, ...), custom_call_target="tpu_custom_call", output_to_operand_aliasing={{2}: (10, {}), {3}: (11, {}), {4}: (12, {}), {5}: (13, {})} | custom-call | flops 1073741824 | bytes 83886080 | tf_op jit(solution)/shard_map/now/pallas_call | solution.py:559
  82.7 7.3 %all-to-all-start.1 = ((s32[8,16,1152]{2,1,0:T(8,128)}), s32[8,16,1152]{2,1,0:T(8,128)S(1)}, u32[]{:S(2)}, u32[]{:S(2)}) async-start(s32[8,16,1152]{2,1,0:T(8,128)} %get-tuple-element.79), calls=%async_computation.1 | async-start | bytes 1179648 | tf_op jit(solution)/shard_map/all_to_all | solution.py:741
  90.1 16.9 %all-to-all-done.1.got_ref = s32[8,16,1152]{2,1,0:T(8,128)S(1)} async-done(((s32[8,16,1152]{2,1,0:T(8,128)}), s32[8,16,1152]{2,1,0:T(8,128)S(1)}, u32[]{:S(2)}, u32[]{:S(2)}) %all-to-all-start.1) | async-done | bytes 589856 | tf_op jit(solution)/shard_map/all_to_all | solution.py:741
  106.9 2.2 %sum.1 = s32[16,1152]{1,0:T(8,128)S(1)} custom-call(s32[8,16,1152]{2,1,0:T(8,128)S(1)} %all-to-all-done.1.got_ref), custom_call_target="tpu_custom_call" | custom-call | tf_op jit(solution)/shard_map/sum/pallas_call | solution.py:604
  109.1 5.9 %all-gather = s32[64,1152]{1,0:T(8,128)S(1)} all-gather(s32[16,1152]{1,0:T(8,128)S(1)} %sum.1), channel_id=2, replica_groups=mesh['row'=4,'col'=8] {'row'}, dimensions={0}, use_global_device_ids=true | all-gather | bytes 368640 | tf_op jit(solution)/shard_map/all_gather | solution.py:743
  115.0 5.1 %drops.1 = f32[32,2048]{1,0:T(8,128)S(1)} custom-call(s32[2,2048]{1,0:T(2,128)S(1)} %bitcast.29, s32[4,16,1152]{2,1,0:T(8,128)S(1)} %bitcast.27), custom_call_target="tpu_custom_call" | custom-call | tf_op jit(solution)/shard_map/drops/pallas_call | solution.py:650
  120.2 12.9 %all_to_all.22 = f32[8,32,256]{2,1,0:T(8,128)S(1)} all-to-all(f32[8,32,256]{2,1,0:T(8,128)S(1)} %bitcast.32), channel_id=1, replica_groups=mesh['row'=4,'col'=8] {'col'}, dimensions={0} | all-to-all | bytes 524288 | tf_op jit(solution)/shard_map/all_to_all | solution.py:747
  133.0 0.8 copy.19
  (26 shorter events, 0.3 us)
Async XLA Ops:
  0.6 1.0 copy-start
  1.7 9.0 %collective-permute-start = (s32[256,128]{1,0:T(8,128)S(1)}, s32[256,128]{1,0:T(8,128)S(1)}, u32[]{:S(2)}, u32[]{:S(2)}) collective-permute-start(s32[256,128]{1,0:T(8,128)S(1)} %get-tuple-element.42), channel_id=1, source_target_pairs={{0,2},{1,3},{2,0},{3,1},{4,6},{5,7},{6,4},{7,5},{8,24},{9,25},{10,... | collective-permute-start | bytes 393224 | tf_op jit(solution)/shard_map/ppermute | solution.py:702
  8.6 0.7 copy-start.3
  9.3 0.7 copy-start.4
  10.8 15.0 %collective-permute-start.1 = (s32[512,128]{1,0:T(8,128)S(1)}, s32[512,128]{1,0:T(8,128)S(1)}, u32[]{:S(2)}, u32[]{:S(2)}) collective-permute-start(s32[512,128]{1,0:T(8,128)S(1)} %pad_add_fusion.2), channel_id=1, source_target_pairs={{0,4},{1,5},{2,6},{3,7},{4,0},{5,1},{6,2},{7,3},{8,10},{9,11},{10,... | collective-permute-start | bytes 786440 | tf_op jit(solution)/shard_map/ppermute | solution.py:702
  25.9 19.8 %collective-permute-start.2 = (s32[1024,128]{1,0:T(8,128)S(1)}, s32[1024,128]{1,0:T(8,128)S(1)}, u32[]{:S(2)}, u32[]{:S(2)}) collective-permute-start(s32[1024,128]{1,0:T(8,128)S(1)} %pad_add_fusion.1), channel_id=1, source_target_pairs={{0,1},{1,0},{2,3},{3,2},{4,5},{5,4},{6,7},{7,6},{8,12},{9,13},{10,... | collective-permute-start | bytes 1572872 | tf_op jit(solution)/shard_map/ppermute | solution.py:702
  28.6 17.1 %all-to-all-start = ((s32[32,16,128]{2,1,0:T(8,128)}), s32[32,16,128]{2,1,0:T(8,128)S(1)}, u32[]{:S(2)}, u32[]{:S(2)}) async-start(s32[32,16,128]{2,1,0:T(8,128)} %bitcast.3), calls=%async_computation | async-start | bytes 524288 | tf_op jit(solution)/shard_map/all_to_all | solution.py:673
  31.2 17.3 %copy-start.1 = (s32[2,16]{1,0:T(2,128)S(1)}, s32[2,16]{1,0:T(2,128)}, u32[]{:S(2)}) copy-start(s32[2,16]{1,0:T(2,128)} %constant.18.clone.mask_ref.refs_1_) | copy-start | bytes 388
  44.0 19.4 %copy-start.2 = (s32[512]{0:T(512)S(1)}, s32[512]{0:T(512)}, u32[]{:S(2)}) copy-start(s32[512]{0:T(512)} %get-tuple-element.62.refs_2_) | copy-start | bytes 6148
  44.0 19.3 %copy-start.5 = (s32[69]{0:T(128)S(1)}, s32[69]{0:T(128)}, u32[]{:S(2)}) copy-start(s32[69]{0:T(128)} %get-tuple-element.63.refs_3_) | copy-start | bytes 832
  45.7 2.7 %collective-permute-start.4 = (s32[2048,128]{1,0:T(8,128)S(1)}, s32[2048,128]{1,0:T(8,128)S(1)}, u32[]{:S(2)}, u32[]{:S(2)}) collective-permute-start(s32[2048,128]{1,0:T(8,128)S(1)} %pad_add_fusion.one_ref), channel_id=1, source_target_pairs={{0,8},{1,9},{2,10},{3,11},{4,12},{5,13},{6,14},{7,15},{8,0},{9,1},... | collective-permute-start | bytes 3145736 | tf_op jit(solution)/shard_map/ppermute | solution.py:720
  45.8 14.9 %collective-permute-start.3 = (s32[2048,128]{1,0:T(8,128)S(1)}, s32[2048,128]{1,0:T(8,128)S(1)}, u32[]{:S(2)}, u32[]{:S(2)}) collective-permute-start(s32[2048,128]{1,0:T(8,128)S(1)} %pad_add_fusion.one_ref), channel_id=1, source_target_pairs={{0,16},{1,17},{2,18},{3,19},{4,20},{5,21},{6,22},{7,23},{8,9},{9,8... | collective-permute-start | bytes 3145736 | tf_op jit(solution)/shard_map/ppermute | solution.py:719
  60.7 2.7 %collective-permute-start.5 = (s32[2048,128]{1,0:T(8,128)S(1)}, s32[2048,128]{1,0:T(8,128)S(1)}, u32[]{:S(2)}, u32[]{:S(2)}) collective-permute-start(s32[2048,128]{1,0:T(8,128)S(1)} %collective-permute-done.3.refs_6_), channel_id=1, source_target_pairs={{0,8},{1,9},{2,10},{3,11},{4,12},{5,13},{6,14},{7,15},{8,0},{9,1},... | collective-permute-start | bytes 3145736 | tf_op jit(solution)/shard_map/ppermute | solution.py:735
  82.7 24.2 %all-to-all-start.1 = ((s32[8,16,1152]{2,1,0:T(8,128)}), s32[8,16,1152]{2,1,0:T(8,128)S(1)}, u32[]{:S(2)}, u32[]{:S(2)}) async-start(s32[8,16,1152]{2,1,0:T(8,128)} %get-tuple-element.79), calls=%async_computation.1 | async-start | bytes 1179648 | tf_op jit(solution)/shard_map/all_to_all | solution.py:741

commit v4 on v3

--- a/solution.py
+++ b/solution.py
@@ -11,7 +11,7 @@
 F32, BF16, I32 = jnp.float32, jnp.bfloat16, jnp.int32
 ALL = ("row", "col")
 CHAINS = 4
-UNROLL = 4
+UNROLL = 8
 GROUP = 4
 LANES = 128
 FULL = 32767.0
@@ -127,8 +127,9 @@
     return log2(chain_rows) + 2
 
 
-def list_kernel(sizes, owner_ref, slot_ref, out_ref, tally_ref):
+def list_kernel(sizes, share, owner_ref, slot_ref, slab_owner_ref, slab_offset_ref, out_ref, tally_ref, slab_ref):
     rows_of, owned, block, capacity, chain_rows = sizes
+    slab_ref[...] = slab_owner_ref[...] * share + slab_offset_ref[...]
     count = owner_ref.shape[1]
     ends = 2 * count
     owner = jnp.concatenate([owner_ref[0:1, :], owner_ref[1:2, :]], axis=1)
@@ -164,15 +165,20 @@
     out_ref[...] = total[: out_ref.shape[0]]
 
 
-def make_lists(owner, slot, sizes, keys):
+def make_lists(owner, slot, slab_owner, slab_offset, share, sizes, keys):
+    arrays = [pltpu.with_memory_space_constraint(x.T, pltpu.HBM) for x in (owner, slot, slab_owner, slab_offset)]
     return pl.pallas_call(
-        functools.partial(list_kernel, sizes),
-        out_shape=(jax.ShapeDtypeStruct((keys, sizes[3]), I32), jax.ShapeDtypeStruct((1, LANES), I32)),
-        in_specs=vmem(2),
-        out_specs=tuple(vmem(2)),
+        functools.partial(list_kernel, sizes, share),
+        out_shape=(
+            jax.ShapeDtypeStruct((keys, sizes[3]), I32),
+            jax.ShapeDtypeStruct((1, LANES), I32),
+            jax.ShapeDtypeStruct(arrays[2].shape, I32),
+        ),
+        in_specs=vmem(4),
+        out_specs=tuple(vmem(3)),
         compiler_params=params(24),
         name="lists",
-    )(owner.T, slot.T)
+    )(*arrays)
 
 
 def routes(row_count, col_count):
@@ -411,9 +417,13 @@
         scatter(sizes, first, skip, batch, lists_ref, mask_ref, rows, acc)
 
 
-def early_kernel(sizes, lists_ref, mask_ref, message_ref, one_ref, two_ref, *more):
-    acc, (codes, rows, head, sems) = more[:CHAINS], more[CHAINS:]
-    copies = [*row_copies((one_ref, two_ref), codes, sems), head_copy(sizes, message_ref, head, sems.at[2])]
+def early_kernel(sizes, flat_ref, mask_ref, message_ref, one_ref, two_ref, *more):
+    acc, (codes, rows, head, lists_ref, sems) = more[:CHAINS], more[CHAINS:]
+    copies = [
+        *row_copies((one_ref, two_ref), codes, sems),
+        head_copy(sizes, message_ref, head, sems.at[2]),
+        pltpu.make_async_copy(flat_ref, lists_ref, sems.at[3]),
+    ]
     for copy in copies:
         copy.start()
     clear = 512
@@ -434,6 +444,7 @@
         pltpu.VMEM((2 * pieces[0].shape[0], LANES), I32),
         pltpu.VMEM((4 * rows, LANES), F32),
         head_shape(sizes, devices),
+        pltpu.SMEM((devices * sizes[1],), I32),
     ], (2 * pieces[0].shape[0] + 4 * rows + devices * 16) * LANES * 4 >> 20
 
 
@@ -444,9 +455,9 @@
     return pl.pallas_call(
         functools.partial(early_kernel, sizes),
         out_shape=tuple(pltpu.VMEM((2 * (nodes // CHAINS + PAD), LANES), F32) for _ in range(CHAINS)),
-        in_specs=[smem] * 2 + [hbm] * 3,
+        in_specs=[hbm, smem] + [hbm] * 3,
         out_specs=tuple(vmem(CHAINS)),
-        scratch_shapes=[*room, pltpu.SemaphoreType.DMA((3,))],
+        scratch_shapes=[*room, pltpu.SemaphoreType.DMA((4,))],
         compiler_params=params(mib + 4),
         cost_estimate=pl.CostEstimate(flops=1 << 28, bytes_accessed=32 << 20, transcendentals=0),
         name="early",
@@ -455,13 +466,17 @@
 
 def now_kernel(
     block, slots, chunks, sizes,
-    lists_ref, mask_ref, todo_ref, owner_ref, past_ref, message_ref,
+    flat_ref, mask_ref, todo_ref, owner_ref, past_ref, message_ref,
     one_ref, two_ref, history_ref, coef_ref,
     charge_ref, out_ref, acc,
-    codes, rows, head, charge, coef, source_of, total, row_sem, load_sem, store_sem, coef_sem,
+    codes, rows, head, lists_ref, charge, coef, source_of, total, row_sem, load_sem, store_sem, coef_sem,
 ):
     row_blocks, col_blocks = total.shape[0], charge.shape[0] // block
-    copies = [*row_copies((one_ref, two_ref), codes, row_sem), head_copy(sizes, message_ref, head, row_sem.at[2])]
+    copies = [
+        *row_copies((one_ref, two_ref), codes, row_sem),
+        head_copy(sizes, message_ref, head, row_sem.at[2]),
+        pltpu.make_async_copy(flat_ref, lists_ref, row_sem.at[3]),
+    ]
     for copy in copies:
         copy.start()
     load = pltpu.make_async_copy(history_ref.at[0], charge, load_sem)
@@ -563,7 +578,7 @@
             jax.ShapeDtypeStruct((chunks, scenarios // chunks // 2, rows + LANES), I32),
             *[pltpu.VMEM(part.shape, F32) for part in acc],
         ),
-        in_specs=[smem] * 4 + vmem(1) + [hbm] * 5 + vmem(count),
+        in_specs=[hbm] + [smem] * 3 + vmem(1) + [hbm] * 5 + vmem(count),
         out_specs=(hbm, *vmem(1 + count)),
         input_output_aliases={before + n: 2 + n for n in range(count)},
         scratch_shapes=[
@@ -572,7 +587,7 @@
             pltpu.VMEM((slots, block, GROUP * block), BF16),
             pltpu.VMEM((GROUP * block, scenarios), BF16),
             pltpu.VMEM((row_blocks, block, scenarios), F32),
-            pltpu.SemaphoreType.DMA((3,)),
+            pltpu.SemaphoreType.DMA((4,)),
             pltpu.SemaphoreType.DMA,
             pltpu.SemaphoreType.DMA,
             pltpu.SemaphoreType.DMA((slots, GROUP)),
@@ -658,8 +673,8 @@
 
 
 def branch_lists(index, owner, slot, slab_owner, slab_offset, col_count, share, sizes):
-    lists, tally = make_lists(owner, slot, sizes, col_count * CHAINS)
-    slab = (slab_owner * share + slab_offset).T.reshape(-1, LANES)
+    lists, tally, slab = make_lists(owner, slot, slab_owner, slab_offset, share, sizes, col_count * CHAINS)
+    slab = slab.reshape(-1, LANES)
     return lists.reshape(col_count, -1, LANES), tally, jnp.concatenate([index, slab], axis=0)
 
 

time: 135 us -> 132 us (0.978)
  Pallas kernels: 65.3 us -> 68.5 us
  waiting for transfers between devices: 25.2 us -> 23.2 us
  starting transfers between devices: 18.8 us -> 17.3 us
  local copies, waits for them, and re-layouts: 4.11 us -> 2.75 us
    unnamed x14 -> x10, local copies, waits for them, and re-layouts: 3.16 us -> 1.81 us
  transfers between devices with their start and end apart: 8 -> 8, of which waited for: 5 -> 5; matrix products, arithmetic and copies ran while one was open for 1% -> 1% of each run, Pallas kernels for 29% -> 31%
where the time goes in v4:
time: 132 us
  Pallas kernels  68.5 us (52%)
  waiting for transfers between devices  23.2 us (18%)
  blocking collectives  18.7 us (14%)
  starting transfers between devices  17.3 us (13%)
  local copies, waits for them, and re-layouts  2.75 us (2%)
    pallas_call x2, Pallas kernels, past_product(): pl.pallas_call(functools.partial(past_kernel, block, slots, region_of(coe...  26.2 us
    pallas_call x1, Pallas kernels, now_product(): pl.pallas_call(kernel, out_shape=(jax.ShapeDtypeStruct((nodes, scenarios)...  20 us
    all_to_all x1, waiting for transfers between devices, local(): lax.all_to_all(partial, 'col', split_axis=0, concat_axis=0, tiled=True)  16.3 us
    all_to_all x1, blocking collectives, local(): lax.all_to_all(found, 'col', split_axis=0, concat_axis=0, tiled=True)  12.9 us
    pallas_call x1, Pallas kernels, early_scatter(): pl.pallas_call(functools.partial(early_kernel, sizes), out_shape=tuple((p...  10.3 us
    ppermute x3, starting transfers between devices, local(): got = lax.ppermute(held, ALL, step)  6.9 us
    all_to_all x1, starting transfers between devices, local(): lax.all_to_all(partial, 'col', split_axis=0, concat_axis=0, tiled=True)  6.13 us
    all_gather x1, blocking collectives, local(): potentials = lax.all_gather(mine, 'row', axis=0, tiled=False)  5.87 us
  transfers between devices with their start and end apart: 8, of which 5 were waited for; matrix products, arithmetic and copies ran while one was open for 1% of the time, Pallas kernels for 31%

profile of v4, /device:TPU:0, one launch (start us, length us, event | category | flops | bytes accessed | tf_op | source)
XLA Modules:
  0.0 131.5 jit_solution(6100387311201744152)
XLA Ops:
  0.6 0.9 copy-done
  1.6 0.1 pack.1
  1.7 3.1 %collective-permute-start = (s32[256,128]{1,0:T(8,128)S(1)}, s32[256,128]{1,0:T(8,128)S(1)}, u32[]{:S(2)}, u32[]{:S(2)}) collective-permute-start(s32[256,128]{1,0:T(8,128)S(1)} %get-tuple-element.43), channel_id=1, source_target_pairs={{0,2},{1,3},{2,0},{3,1},{4,6},{5,7},{6,4},{7,5},{8,24},{9,25},{10,... | collective-permute-start | bytes 393224 | tf_op jit(solution)/shard_map/ppermute | solution.py:717
  4.8 1.4 %lists.1 = (s32[32,256]{1,0:T(8,128)S(1)}, s32[1,128]{1,0:T(1,128)S(1)}, s32[2,256]{1,0:T(2,128)S(1)}) custom-call(s32[2,256]{1,0:T(2,128)} %bitcast.33, s32[2,256]{1,0:T(2,128)} %bitcast.34, s32[2,256]{1,0:T(2,128)} %bitcast.35, s32[2,256]{1,0:T(2,128)} %bitcast.36), custom_call_target="tpu_custom_call" | custom-call | tf_op jit(solution)/shard_map/lists/pallas_call | solution.py:170
  6.2 3.1 %scan.1 = (s32[512]{0:T(512)}, s32[69]{0:T(128)}, s32[512]{0:T(512)}, s32[69]{0:T(128)}) custom-call(s32[4,64]{1,0:T(4,128)} %delays_ref.1), custom_call_target="tpu_custom_call" | custom-call | tf_op jit(solution)/shard_map/scan/pallas_call | solution.py:340
  9.4 0.1 pad.6.clone
  9.5 2.6 %collective-permute-start.1 = (s32[512,128]{1,0:T(8,128)S(1)}, s32[512,128]{1,0:T(8,128)S(1)}, u32[]{:S(2)}, u32[]{:S(2)}) collective-permute-start(s32[512,128]{1,0:T(8,128)S(1)} %pad_add_fusion.2), channel_id=1, source_target_pairs={{0,4},{1,5},{2,6},{3,7},{4,0},{5,1},{6,2},{7,3},{8,10},{9,11},{10,... | collective-permute-start | bytes 786440 | tf_op jit(solution)/shard_map/ppermute | solution.py:717
  12.1 0.1 broadcast_in_dim.8.start_ref
  12.2 13.0 %past.2.start_ref = f32[4,256,256]{2,1,0:T(8,128)S(1)} custom-call(s32[512]{0:T(512)} %get-tuple-element.53.todo_ref, s32[69]{0:T(128)} %get-tuple-element.54.owner_ref, f32[4,256,256]{2,1,0:T(8,128)S(1)} %broadcast_in_dim.8.start_ref, bf16[4,16384,256]{2,1,0:T(8,128)(2,1)} %refs_8_.1, bf16[1024,16384]{1,0:T(8,128)(2,1)} %refs_9_.1), custom_call_target="tpu_custom_call" | custom-call | flops 4294967296 | bytes 33554432 | tf_op jit(solution)/shard_map/past/pallas_call | solution.py:278
  25.2 0.1 add_add_fusion
  25.3 1.2 collective-permute-start.2
  26.5 0.7 broadcast_in_dim.21
  27.2 2.6 %all-to-all-start = ((s32[32,16,128]{2,1,0:T(8,128)}), s32[32,16,128]{2,1,0:T(8,128)S(1)}, u32[]{:S(2)}, u32[]{:S(2)}) async-start(s32[32,16,128]{2,1,0:T(8,128)} %bitcast.4), calls=%async_computation | async-start | bytes 524288 | tf_op jit(solution)/shard_map/all_to_all | solution.py:688
  29.8 0.0 copy-start.1
  29.8 13.2 %past.3.refs_4_ = f32[4,256,256]{2,1,0:T(8,128)S(1)} custom-call(s32[512]{0:T(512)} %get-tuple-element.53.todo_ref, s32[69]{0:T(128)} %get-tuple-element.54.owner_ref, f32[4,256,256]{2,1,0:T(8,128)S(1)} %past.2.start_ref, bf16[4,16384,256]{2,1,0:T(8,128)(2,1)} %refs_8_.1, bf16[1024,16384]{1,0:T(8,128)(2,1)} %refs_9_.1), custom_call_target="tpu_custom_call" | custom-call | flops 4294967296 | bytes 33554432 | tf_op jit(solution)/shard_map/past/pallas_call | solution.py:278
  43.1 0.0 copy-start.2
  43.1 1.2 all-to-all-done
  44.3 0.1 pad_add_fusion.one_ref
  44.4 0.1 collective-permute-start.4
  44.5 1.6 %collective-permute-start.3 = (s32[2048,128]{1,0:T(8,128)S(1)}, s32[2048,128]{1,0:T(8,128)S(1)}, u32[]{:S(2)}, u32[]{:S(2)}) collective-permute-start(s32[2048,128]{1,0:T(8,128)S(1)} %pad_add_fusion.one_ref), channel_id=1, source_target_pairs={{0,16},{1,17},{2,18},{3,19},{4,20},{5,21},{6,22},{7,23},{8,9},{9,8... | collective-permute-start | bytes 3145736 | tf_op jit(solution)/shard_map/ppermute | solution.py:734
  46.1 1.0 collective-permute-done.4.two_ref
  47.1 10.3 %early.1 = (f32[8200,128]{1,0:T(8,128)S(1)}, f32[8200,128]{1,0:T(8,128)S(1)}, f32[8200,128]{1,0:T(8,128)S(1)}, f32[8200,128]{1,0:T(8,128)S(1)}) custom-call(s32[65536]{0:T(1024)S(1)} %bitcast.25, s32[2,16]{1,0:T(2,128)S(1)} %copy-done.1, s32[32,16,128]{2,1,0:T(8,128)S(1)} %all-to-all-done, s32[2048,128]{1,0:T(8,128)S(1)} %pad_add_fusion.one_ref, ...), custom_call_target="tpu_custom_call" | custom-call | flops 268435456 | bytes 33554432 | tf_op jit(solution)/shard_map/early/pallas_call | solution.py:455
  57.4 1.9 %collective-permute-done.3.refs_6_ = s32[2048,128]{1,0:T(8,128)S(1)} collective-permute-done((s32[2048,128]{1,0:T(8,128)S(1)}, s32[2048,128]{1,0:T(8,128)S(1)}, u32[]{:S(2)}, u32[]{:S(2)}) %collective-permute-start.3) | collective-permute-done | bytes 1048608 | tf_op jit(solution)/shard_map/ppermute | solution.py:734
  59.3 2.7 %collective-permute-done.5.refs_7_ = s32[2048,128]{1,0:T(8,128)S(1)} collective-permute-done((s32[2048,128]{1,0:T(8,128)S(1)}, s32[2048,128]{1,0:T(8,128)S(1)}, u32[]{:S(2)}, u32[]{:S(2)}) %collective-permute-start.5) | collective-permute-done | bytes 1048608 | tf_op jit(solution)/shard_map/ppermute | solution.py:750
  62.0 20.0 %now.1 = (bf16[16384,256]{1,0:T(8,128)(2,1)}, s32[8,16,1152]{2,1,0:T(8,128)}, f32[8200,128]{1,0:T(8,128)S(1)}, f32[8200,128]{1,0:T(8,128)S(1)}, f32[8200,128]{1,0:T(8,128)S(1)}, /*index=5*/f32[8200,128]{1,0:T(8,128)S(1)}) custom-call(s32[65536]{0:T(1024)S(1)} %bitcast.26, ...), custom_call_target="tpu_custom_call", output_to_operand_aliasing={{2}: (10, {}), {3}: (11, {}), {4}: (12, {}), {5}: (13, {})} | custom-call | flops 1073741824 | bytes 83886080 | tf_op jit(solution)/shard_map/now/pallas_call | solution.py:574
  82.0 6.1 %all-to-all-start.1 = ((s32[8,16,1152]{2,1,0:T(8,128)}), s32[8,16,1152]{2,1,0:T(8,128)S(1)}, u32[]{:S(2)}, u32[]{:S(2)}) async-start(s32[8,16,1152]{2,1,0:T(8,128)} %get-tuple-element.81), calls=%async_computation.1 | async-start | bytes 1179648 | tf_op jit(solution)/shard_map/all_to_all | solution.py:756
  88.2 16.3 %all-to-all-done.1.got_ref = s32[8,16,1152]{2,1,0:T(8,128)S(1)} async-done(((s32[8,16,1152]{2,1,0:T(8,128)}), s32[8,16,1152]{2,1,0:T(8,128)S(1)}, u32[]{:S(2)}, u32[]{:S(2)}) %all-to-all-start.1) | async-done | bytes 589856 | tf_op jit(solution)/shard_map/all_to_all | solution.py:756
  104.6 2.2 %sum.1 = s32[16,1152]{1,0:T(8,128)S(1)} custom-call(s32[8,16,1152]{2,1,0:T(8,128)S(1)} %all-to-all-done.1.got_ref), custom_call_target="tpu_custom_call" | custom-call | tf_op jit(solution)/shard_map/sum/pallas_call | solution.py:619
  106.8 5.9 %all-gather = s32[64,1152]{1,0:T(8,128)S(1)} all-gather(s32[16,1152]{1,0:T(8,128)S(1)} %sum.1), channel_id=2, replica_groups=mesh['row'=4,'col'=8] {'row'}, dimensions={0}, use_global_device_ids=true | all-gather | bytes 368640 | tf_op jit(solution)/shard_map/all_gather | solution.py:758
  112.6 5.1 %drops.1 = f32[32,2048]{1,0:T(8,128)S(1)} custom-call(s32[2,2048]{1,0:T(2,128)S(1)} %bitcast.29, s32[4,16,1152]{2,1,0:T(8,128)S(1)} %bitcast.27), custom_call_target="tpu_custom_call" | custom-call | tf_op jit(solution)/shard_map/drops/pallas_call | solution.py:665
  117.8 12.9 %all_to_all.22 = f32[8,32,256]{2,1,0:T(8,128)S(1)} all-to-all(f32[8,32,256]{2,1,0:T(8,128)S(1)} %bitcast.30), channel_id=1, replica_groups=mesh['row'=4,'col'=8] {'col'}, dimensions={0} | all-to-all | bytes 524288 | tf_op jit(solution)/shard_map/all_to_all | solution.py:762
  130.7 0.8 copy.19
  (21 shorter events, 0.2 us)
Async XLA Ops:
  0.6 1.0 copy-start
  1.7 7.7 %collective-permute-start = (s32[256,128]{1,0:T(8,128)S(1)}, s32[256,128]{1,0:T(8,128)S(1)}, u32[]{:S(2)}, u32[]{:S(2)}) collective-permute-start(s32[256,128]{1,0:T(8,128)S(1)} %get-tuple-element.43), channel_id=1, source_target_pairs={{0,2},{1,3},{2,0},{3,1},{4,6},{5,7},{6,4},{7,5},{8,24},{9,25},{10,... | collective-permute-start | bytes 393224 | tf_op jit(solution)/shard_map/ppermute | solution.py:717
  9.5 15.8 %collective-permute-start.1 = (s32[512,128]{1,0:T(8,128)S(1)}, s32[512,128]{1,0:T(8,128)S(1)}, u32[]{:S(2)}, u32[]{:S(2)}) collective-permute-start(s32[512,128]{1,0:T(8,128)S(1)} %pad_add_fusion.2), channel_id=1, source_target_pairs={{0,4},{1,5},{2,6},{3,7},{4,0},{5,1},{6,2},{7,3},{8,10},{9,11},{10,... | collective-permute-start | bytes 786440 | tf_op jit(solution)/shard_map/ppermute | solution.py:717
  25.3 19.0 %collective-permute-start.2 = (s32[1024,128]{1,0:T(8,128)S(1)}, s32[1024,128]{1,0:T(8,128)S(1)}, u32[]{:S(2)}, u32[]{:S(2)}) collective-permute-start(s32[1024,128]{1,0:T(8,128)S(1)} %pad_add_fusion.1), channel_id=1, source_target_pairs={{0,1},{1,0},{2,3},{3,2},{4,5},{5,4},{6,7},{7,6},{8,12},{9,13},{10,... | collective-permute-start | bytes 1572872 | tf_op jit(solution)/shard_map/ppermute | solution.py:717
  27.2 17.1 %all-to-all-start = ((s32[32,16,128]{2,1,0:T(8,128)}), s32[32,16,128]{2,1,0:T(8,128)S(1)}, u32[]{:S(2)}, u32[]{:S(2)}) async-start(s32[32,16,128]{2,1,0:T(8,128)} %bitcast.4), calls=%async_computation | async-start | bytes 524288 | tf_op jit(solution)/shard_map/all_to_all | solution.py:688
  29.8 17.3 %copy-start.1 = (s32[2,16]{1,0:T(2,128)S(1)}, s32[2,16]{1,0:T(2,128)}, u32[]{:S(2)}) copy-start(s32[2,16]{1,0:T(2,128)} %constant.16.clone.mask_ref.refs_1_) | copy-start | bytes 388
  43.1 18.9 %copy-start.2 = (s32[512]{0:T(512)S(1)}, s32[512]{0:T(512)}, u32[]{:S(2)}) copy-start(s32[512]{0:T(512)} %get-tuple-element.64.refs_2_) | copy-start | bytes 6148
  43.1 18.9 %copy-start.3 = (s32[69]{0:T(128)S(1)}, s32[69]{0:T(128)}, u32[]{:S(2)}) copy-start(s32[69]{0:T(128)} %get-tuple-element.65.refs_3_) | copy-start | bytes 832
  44.4 2.7 %collective-permute-start.4 = (s32[2048,128]{1,0:T(8,128)S(1)}, s32[2048,128]{1,0:T(8,128)S(1)}, u32[]{:S(2)}, u32[]{:S(2)}) collective-permute-start(s32[2048,128]{1,0:T(8,128)S(1)} %pad_add_fusion.one_ref), channel_id=1, source_target_pairs={{0,8},{1,9},{2,10},{3,11},{4,12},{5,13},{6,14},{7,15},{8,0},{9,1},... | collective-permute-start | bytes 3145736 | tf_op jit(solution)/shard_map/ppermute | solution.py:735
  44.5 14.9 %collective-permute-start.3 = (s32[2048,128]{1,0:T(8,128)S(1)}, s32[2048,128]{1,0:T(8,128)S(1)}, u32[]{:S(2)}, u32[]{:S(2)}) collective-permute-start(s32[2048,128]{1,0:T(8,128)S(1)} %pad_add_fusion.one_ref), channel_id=1, source_target_pairs={{0,16},{1,17},{2,18},{3,19},{4,20},{5,21},{6,22},{7,23},{8,9},{9,8... | collective-permute-start | bytes 3145736 | tf_op jit(solution)/shard_map/ppermute | solution.py:734
  59.3 2.7 %collective-permute-start.5 = (s32[2048,128]{1,0:T(8,128)S(1)}, s32[2048,128]{1,0:T(8,128)S(1)}, u32[]{:S(2)}, u32[]{:S(2)}) collective-permute-start(s32[2048,128]{1,0:T(8,128)S(1)} %collective-permute-done.3.refs_6_), channel_id=1, source_target_pairs={{0,8},{1,9},{2,10},{3,11},{4,12},{5,13},{6,14},{7,15},{8,0},{9,1},... | collective-permute-start | bytes 3145736 | tf_op jit(solution)/shard_map/ppermute | solution.py:750
  82.0 22.5 %all-to-all-start.1 = ((s32[8,16,1152]{2,1,0:T(8,128)}), s32[8,16,1152]{2,1,0:T(8,128)S(1)}, u32[]{:S(2)}, u32[]{:S(2)}) async-start(s32[8,16,1152]{2,1,0:T(8,128)} %get-tuple-element.81), calls=%async_computation.1 | async-start | bytes 1179648 | tf_op jit(solution)/shard_map/all_to_all | solution.py:756
